TPU v7x, 256 devices: a whole 4x4x8 slice. The times are simulated.
256 devices in a mesh: src: 32 (over y, x, core), tgt: 8 (over z).
Axes of the slice: x: 4, y: 4, z: 8, core: 2. Of those that a mesh axis runs over, the one named last changes fastest.
Arguments:
- src_points: bfloat16 [32, 524288], P(None, 'src'), may hold values from -24 to 24
- tgt_points: bfloat16 [32, 524288], P(None, 'tgt'), may hold values from -6 to 6
- tgt_potential: float32 [524288], P('tgt'), may hold values from -2 to 2
- support: int32 [4096, 8, 6], P('src', 'tgt'), may hold values from 0 to 511, as said below
- counts: int32 [4096, 8], P('src', 'tgt'), may hold values from 1 to 6, as said below
Outputs:
- src_potential: float32 [524288], P('src')
- new_tgt_potential: float32 [524288], P('tgt')
Inputs may be any that keep to these rules, and one draw needn't show every extreme that they name: support[r, t, k] names target block t * 512 + support[r, t, k]; the first counts[r, t] entries of a list are distinct; every target block is named in the used part of some list. `counts`: for every source block the list of some target shard is full.
All inputs are finite; a program needn't handle non-finite values.
Results may differ from a plain program's by a relative error of at most 0.0004.
Values sent between devices are 32-bit elements; how exact they have to be, the bound alone decides.
A program may use at most 128 MiB of HBM per device.

v0:
```python
import math

import jax
import jax.numpy as jnp
from jax import lax
from jax.sharding import PartitionSpec as P

BLK = 128


entropy_blur = 0.05
neg_fill = -1e30


def body(src_points, tgt_points, tgt_potential, support, counts):
    features = src_points.shape[0]
    src_count = src_points.shape[1]
    tgt_count = tgt_points.shape[1]
    src_blocks = src_count // BLK
    tgt_blocks = tgt_count // BLK
    slot_count = support.shape[2]
    total_src = src_count * lax.axis_size("src")
    total_tgt = tgt_count * lax.axis_size("tgt")
    per_step = math.gcd(src_blocks, 8)
    step_count = src_blocks // per_step
    block_lists = support[:, 0, :]
    live_slots = jnp.arange(slot_count, dtype=jnp.int32)[None, :] < counts[:, 0][:, None]
    src_sq = jnp.sum(jnp.square(src_points.astype(jnp.float32)), axis=0).reshape(src_blocks, BLK)
    tgt_cube = tgt_points.reshape(features, tgt_blocks, BLK)
    tgt_sq = jnp.sum(jnp.square(tgt_points.astype(jnp.float32)), axis=0).reshape(tgt_blocks, BLK)
    tgt_pot = tgt_potential.reshape(tgt_blocks, BLK)

    def group_cost(step_index):
        first_block = step_index * per_step
        src_rows = lax.dynamic_slice_in_dim(src_points, first_block * BLK, per_step * BLK, 1)
        src_rows = src_rows.reshape(features, per_step, BLK)
        picked = lax.dynamic_slice_in_dim(block_lists, first_block, per_step, 0)
        live_mask = lax.dynamic_slice_in_dim(live_slots, first_block, per_step, 0)
        rows_sq = lax.dynamic_slice_in_dim(src_sq, first_block, per_step, 0)
        near_points = jnp.take(tgt_cube, picked.reshape(-1), axis=1).reshape(
            features, per_step, slot_count, BLK
        )
        inner_prod = jnp.einsum(
            "dgi,dgkj->gikj", src_rows, near_points, preferred_element_type=jnp.float32
        )
        cost_tile = (rows_sq[:, :, None, None] + tgt_sq[picked][:, None, :, :]) / (
            2.0 * features
        ) - inner_prod / features
        return (cost_tile, picked, live_mask)

    def row_part(step_index):
        cost_tile, picked, live_mask = group_cost(step_index)
        row_score = jnp.where(
            live_mask[:, None, :, None],
            (tgt_pot[picked][:, None, :, :] - cost_tile) / entropy_blur,
            neg_fill,
        )
        highest = jnp.max(row_score, axis=(2, 3))
        summed = jnp.sum(jnp.exp(row_score - highest[:, :, None, None]), axis=(2, 3))
        return (highest, summed)

    row_high, row_total = lax.map(row_part, jnp.arange(step_count, dtype=jnp.int32))
    row_high = row_high.reshape(src_count)
    row_total = row_total.reshape(src_count)
    global_high = lax.pmax(row_high, "tgt")
    row_total = lax.psum(row_total * jnp.exp(row_high - global_high), "tgt")
    row_high = global_high
    src_potential = -entropy_blur * (row_high + jnp.log(row_total) - math.log(total_tgt))
    src_pot = src_potential.reshape(src_blocks, BLK)

    def col_part(step_index):
        cost_tile, picked, live_mask = group_cost(step_index)
        block_pot = lax.dynamic_slice_in_dim(src_pot, step_index * per_step, per_step, 0)
        col_score = jnp.where(
            live_mask[:, None, :, None],
            (block_pot[:, :, None, None] - cost_tile) / entropy_blur,
            neg_fill,
        )
        highest = jnp.max(col_score, axis=1)
        summed = jnp.sum(jnp.exp(col_score - highest[:, None]), axis=1)
        return (highest, summed)

    tile_high, tile_total = lax.map(col_part, jnp.arange(step_count, dtype=jnp.int32))
    tile_high = tile_high.reshape(src_blocks * slot_count, BLK)
    tile_total = tile_total.reshape(src_blocks * slot_count, BLK)
    owners = jnp.where(live_slots, block_lists, tgt_blocks).reshape(-1)
    seg_high = jax.ops.segment_max(tile_high, owners, num_segments=tgt_blocks + 1)
    seg_total = jax.ops.segment_sum(
        tile_total * jnp.exp(tile_high - seg_high[owners]), owners, num_segments=tgt_blocks + 1
    )
    col_high = jnp.maximum(seg_high[:tgt_blocks], neg_fill).reshape(tgt_count)
    col_total = seg_total[:tgt_blocks].reshape(tgt_count)
    global_high = lax.pmax(col_high, "src")
    global_total = lax.psum(col_total * jnp.exp(col_high - global_high), "src")
    new_tgt_potential = -entropy_blur * (global_high + jnp.log(global_total) - math.log(total_src))
    return (src_potential, new_tgt_potential)


def solution(mesh):
    return jax.shard_map(
        body,
        mesh=mesh,
        in_specs=(P(None, "src"), P(None, "tgt"), P("tgt"), P("src", "tgt", None), P("src", "tgt")),
        out_specs=(P("src"), P("tgt")),
        check_vma=False,
    )
```

profile of v0, /device:TPU:1, one launch (start us, length us, event | category | flops | bytes accessed | tf_op | source)
XLA Modules:
  0.0 693.1 jit_solution(16128332528436720844)
XLA Ops:
  7.2 5.0 copy_bitcast_fusion
  14.0 156.2 %while.28 = (s32[]{:T(128)}, f32[16,8,128]{2,1,0:T(8,128)S(1)}, f32[16,8,128]{2,1,0:T(8,128)S(1)}, s32[16]{0:T(128)S(1)}, pred[128,6]{1,0:T(8,128)(4,1)S(1)}, /*...) while((s32[]{:T(128)}, f32[16,8,128]{2,1,0:T(8,128)S(1)}, ...), condition=%wide.region_5.7_spmd, body=%wide.region_2.6_spmd.sunk | while | flops 58393160 | bytes 8883529 | solution.py:62
  15.4 2.8 gather_fusion
  20.4 3.0 fusion.24
  25.2 2.8 gather_fusion
  30.1 3.0 fusion.24
  34.9 2.8 gather_fusion
  39.9 3.0 fusion.24
  44.7 2.8 gather_fusion
  49.7 3.0 fusion.24
  54.5 2.8 gather_fusion
  59.4 3.0 fusion.24
  64.2 2.8 gather_fusion
  69.2 3.0 fusion.24
  74.0 2.8 gather_fusion
  78.9 3.0 fusion.24
  88.7 3.0 fusion.24
  98.5 3.0 fusion.24
  108.2 3.0 fusion.24
  118.0 3.0 fusion.24
  127.8 3.0 fusion.24
  137.5 3.0 fusion.24
  147.3 3.0 fusion.24
  157.0 3.0 fusion.24
  166.8 3.0 fusion.24
  171.3 70.0 %all-reduce.5.cloned.1.call-done = f32[16384]{0:T(1024)} async-done(((f32[16384]{0:T(1024)}), f32[16384]{0:T(1024)}) %all-reduce.5.cloned.1.call-update) | async-done | bytes 65552 | tf_op jit(solution)/shard_map/pmax | solution.py:65
  242.8 71.3 %all-reduce.7.cloned.1.call-done = f32[16384]{0:T(1024)} async-done(((f32[16384]{0:T(1024)}), f32[16384]{0:T(1024)}) %all-reduce.7.cloned.1.call-update) | async-done | bytes 65552 | tf_op jit(solution)/shard_map/psum | solution.py:66
  315.0 133.0 %while.29 = (s32[]{:T(128)}, f32[16,8,6,128]{3,2,1,0:T(8,128)S(1)}, f32[16,8,6,128]{3,2,1,0:T(8,128)S(1)}, s32[16]{0:T(128)S(1)}, pred[128,6]{1,0:T(8,128)(4,1)S...) while((s32[]{:T(128)}, f32[16,8,6,128]{3,2,1,0:T(8,128)S(1)}, ...), condition=%wide.region_11.13_spmd, body=%wide.region_8.12_spmd.sunk | while | flops 58382920 | bytes 8948877 | solution.py:83
  448.1 6.1 scatter_custom_fusion
  455.2 9.2 %scatter_custom_fusion.1 = f32[513,128]{1,0:T(8,128)S(1)} fusion(s32[768]{0:T(1024)S(1)} %get-tuple-element.306, f32[768,128]{1,0:T(8,128)S(1)} %reshape.162, f32[768,128]{1,0:T(8,128)S(1)} %reshape.216, f32[]{:T(128)} %constant.183.clone.1, f32[513,128]{1,0:T(8,128)S(1)} %scatter_custom_fusion, s32[1024]{0:T(1024)S(1)} %pad_clamp_fusion.4), kind=kCustom, calls=%fused_computation.42 | custom fusion | flops 294912 | bytes 1319428 | tf_op jit(solution)/shard_map/scatter-add | solution.py:88
  464.4 105.5 %all-reduce.9.cloned.1.call-done = f32[65536]{0:T(1024)} async-done(((f32[65536]{0:T(1024)}), f32[65536]{0:T(1024)}) %all-reduce.9.cloned.1.call-update) | async-done | bytes 262160 | tf_op jit(solution)/shard_map/pmax | solution.py:93
  571.7 113.1 %all-reduce.11.cloned.1.call-done = f32[65536]{0:T(1024)} async-done(((f32[65536]{0:T(1024)}), f32[65536]{0:T(1024)}) %all-reduce.11.cloned.1.call-update) | async-done | bytes 262160 | tf_op jit(solution)/shard_map/psum | solution.py:94
  (676 shorter events, 186.7 us)
Async XLA Ops:
  7.2 234.0 %all-reduce.5.cloned.1.call-start = ((), (), s32[]{:S(2)}) async-start(), calls=%async_computation | async-start | bytes 131072 | tf_op jit(solution)/shard_map/pmax | solution.py:65
  7.2 5.0 copy-start
  12.2 1.3 copy-start.5
  12.2 1.4 copy-start.6
  12.2 1.5 copy-start.2
  12.2 1.8 copy-start.1
  170.2 0.6 copy-start.3
  170.9 143.2 %all-reduce.7.cloned.1.call-start = ((), (), s32[]{:S(2)}) async-start(), calls=%async_computation.1 | async-start | bytes 131072 | tf_op jit(solution)/shard_map/psum | solution.py:66
  242.8 327.2 %all-reduce.9.cloned.1.call-start = ((), (), s32[]{:S(2)}) async-start(), calls=%async_computation.2 | async-start | bytes 524288 | tf_op jit(solution)/shard_map/pmax | solution.py:93
  448.0 238.6 %copy-start.4 = (f32[128,128]{1,0:T(8,128)}, f32[128,128]{1,0:T(8,128)S(1)}, u32[]{:S(2)}) copy-start(f32[128,128]{1,0:T(8,128)S(1)} %get-tuple-element.643) | copy-start | bytes 196612
  454.9 229.9 %all-reduce.11.cloned.1.call-start = ((), (), s32[]{:S(2)}) async-start(), calls=%async_computation.3 | async-start | bytes 524288 | tf_op jit(solution)/shard_map/psum | solution.py:94
Sparse Core Ops, SparseCore 0:
  171.0 70.1 all-reduce.4
  244.2 69.8 all-reduce.6
  455.0 114.8 all-reduce.8
  573.6 111.1 all-reduce.10
where the time goes:
time: 695 us; the launch traced here: 693 us
  waiting for transfers between devices  360 us (52%)
  local copies, waits for them, and re-layouts  150 us (22%)
  matrix products  76.1 us (11%)
  other arithmetic  47.1 us (7%)
  loops' own time  45.3 us (7%)
  between operations  14 us (2%)
    psum x1, waiting for transfers between devices, body(): global_total = lax.psum(col_total * jnp.exp(col_high - global_high), 'src')  113 us
    pmax x1, waiting for transfers between devices, body(): global_high = lax.pmax(col_high, 'src')  106 us
    gather x32, local copies, waits for them, and re-layouts, group_cost(): jnp.take(tgt_cube, picked.reshape(-1), axis=1)  90 us
    dot_general x32, matrix products, group_cost(): jnp.einsum('dgi,dgkj->gikj', src_rows, near_points, preferred_element_typ...  76.1 us
    psum x1, waiting for transfers between devices, body(): row_total = lax.psum(row_total * jnp.exp(row_high - global_high), 'tgt')  71.3 us
    pmax x1, waiting for transfers between devices, body(): global_high = lax.pmax(row_high, 'tgt')  70 us
    another operation x1, loops' own time, body(): lax.map(col_part, jnp.arange(step_count, dtype=jnp.int32))  22.7 us
    another operation x1, loops' own time, body(): lax.map(row_part, jnp.arange(step_count, dtype=jnp.int32))  22.6 us
  transfers between devices with their start and end apart: 4, of which 4 were waited for; matrix products, arithmetic and copies ran while one was open for 1% of the time, Pallas kernels for 0%

commit v1 on v0

v1 whole, which is shorter than its diff:
```python
import functools
import math

import jax
import jax.numpy as jnp
from jax import lax
from jax.experimental import pallas as pl
from jax.experimental.pallas import tpu as pltpu
from jax.sharding import PartitionSpec as P

BLK = 128
BLUR = 0.05
NEG = -1e30
TO_LOG2 = math.log2(math.e) / BLUR
FROM_LOG2 = BLUR * math.log(2.0)
DEPTH = 80
GROUP = 4
F32 = jnp.float32
BF16 = jnp.bfloat16
MESH = pl.DeviceIdType.MESH


def three_parts(v):
    hi = v.astype(BF16).astype(F32)
    mid = (v - hi).astype(BF16).astype(F32)
    return hi, mid, v - hi - mid


def source_rows(x, scale, extra):
    scaled = x.astype(F32) * scale
    hi = scaled.astype(BF16).astype(F32)
    pad = jnp.zeros((BLK - 2 * x.shape[0] - 8, BLK), F32)
    stacked = jnp.concatenate([hi, scaled - hi, extra, pad], axis=0)
    return stacked.T.astype(BF16)[:, :DEPTH]


def sort_by_count(counts_ref, order_ref, start_ref, blocks, slots):
    for c in range(slots + 1):
        start_ref[c] = 0

    def tally(r, _):
        c = counts_ref[r]
        start_ref[c] = start_ref[c] + 1
        return 0

    lax.fori_loop(0, blocks, tally, 0)
    total = 0
    for c in range(1, slots + 1):
        here = start_ref[c]
        start_ref[c] = total
        total = total + here

    def place(r, _):
        c = counts_ref[r]
        at = start_ref[c]
        order_ref[at] = r
        start_ref[c] = at + 1
        return 0

    lax.fori_loop(0, blocks, place, 0)


def by_group(counts_ref, order_ref, blocks, slots, work):
    def step(g, _):
        rows = [order_ref[g * GROUP + q] for q in range(GROUP)]
        most = counts_ref[rows[-1]]
        for c in range(1, slots + 1):
            pl.when(most == c)(functools.partial(work, rows, c))
        return 0

    lax.fori_loop(0, blocks // GROUP, step, 0)


def lane_block(ref, index):
    return ref[:, pl.ds(pl.multiple_of(index * BLK, BLK), BLK)]


def row_kernel(support_ref, counts_ref, x_ref, y_ref, g_ref, out_ref, order_ref, start_ref, extra_ref, score_ref):
    blocks = out_ref.shape[0]
    slots = support_ref.shape[0] // blocks
    features = x_ref.shape[0]
    tgt_blocks = g_ref.shape[0]
    sort_by_count(counts_ref, order_ref, start_ref, blocks, slots)
    sub = lax.broadcasted_iota(jnp.int32, (16, BLK), 0)

    def prepare(step, _):
        wide = y_ref[:, pl.ds(pl.multiple_of(step * 8 * BLK, 8 * BLK), 8 * BLK)].astype(F32)
        sq = jnp.sum(wide * wide, axis=0, keepdims=True)
        pot = g_ref[pl.ds(pl.multiple_of(step * 8, 8), 8), :]
        for q in range(8):
            bias = TO_LOG2 * pot[q : q + 1] - (TO_LOG2 / (2 * features)) * sq[:, q * BLK : (q + 1) * BLK]
            hi, mid, lo = three_parts(bias)
            rows = jnp.where(sub == 0, hi, jnp.where(sub == 1, mid, jnp.where(sub == 2, lo, 0.0)))
            extra_ref[step * 8 + q] = rows.astype(BF16)
        return 0

    lax.fori_loop(0, tgt_blocks // 8, prepare, 0)
    extra_ref[tgt_blocks] = jnp.where(sub == 0, NEG, 0.0).astype(BF16)
    ones = jnp.where(lax.broadcasted_iota(jnp.int32, (8, BLK), 0) < 3, 1.0, 0.0)
    lane = lax.broadcasted_iota(jnp.int32, (BLK, BLK), 1)
    diagonal = lane == lax.broadcasted_iota(jnp.int32, (BLK, BLK), 0)

    def work(rows, c):
        highs = []
        for q, r in enumerate(rows):
            left = source_rows(lane_block(x_ref, r), TO_LOG2 / features, ones)
            live = counts_ref[r]
            high = None
            for k in range(c):
                t = support_ref[r * slots + k]
                y = lane_block(y_ref, t)
                right = jnp.concatenate([y, y, extra_ref[jnp.where(k < live, t, tgt_blocks)]], axis=0)
                score = jnp.dot(left, right, preferred_element_type=F32)
                score_ref[q * slots + k] = score
                high = score if high is None else jnp.maximum(high, score)
            highs.append(jnp.max(high, axis=1, keepdims=True))
        for q, r in enumerate(rows):
            total = None
            for k in range(c):
                term = jnp.exp2(score_ref[q * slots + k] - highs[q])
                total = term if total is None else total + term
            lse = highs[q] + jnp.log2(jnp.sum(total, axis=1, keepdims=True))
            flat = jnp.sum(jnp.where(diagonal, lse, 0.0), axis=0, keepdims=True)
            out_ref[pl.ds(r, 1), :] = flat

    by_group(counts_ref, order_ref, blocks, slots, work)


def col_kernel(log_total, support_ref, counts_ref, x_ref, y_ref, lse_ref, pot_ref, out_ref, order_ref, start_ref, high_ref, total_ref):
    blocks = lse_ref.shape[0]
    slots = support_ref.shape[0] // blocks
    features = x_ref.shape[0]
    tgt_blocks = out_ref.shape[0]
    sort_by_count(counts_ref, order_ref, start_ref, blocks, slots)

    def clear(step, _):
        at = pl.ds(pl.multiple_of(step * 64, 64), 64)
        high_ref[at, :] = jnp.full((64, BLK), NEG, F32)
        total_ref[at, :] = jnp.zeros((64, BLK), F32)
        return 0

    lax.fori_loop(0, high_ref.shape[0] // 64, clear, 0)
    pad_ones = jnp.where(lax.broadcasted_iota(jnp.int32, (16, BLK), 0) < 3, 1.0, 0.0).astype(BF16)
    sub = lax.broadcasted_iota(jnp.int32, (8, BLK), 0)

    def work(rows, c):
        for r in rows:
            x = lane_block(x_ref, r)
            xf = x.astype(F32)
            pot = -FROM_LOG2 * lse_ref[pl.ds(r, 1), :] + BLUR * log_total
            pot_ref[pl.ds(r, 1), :] = pot + jnp.sum(xf * xf, axis=0, keepdims=True) * (1.0 / (2 * features))
            hi, mid, lo = three_parts(TO_LOG2 * pot)
            extra = jnp.where(sub == 0, hi, jnp.where(sub == 1, mid, jnp.where(sub == 2, lo, 0.0)))
            left = source_rows(x, TO_LOG2 / features, extra)
            live = counts_ref[r]
            places, news_high, news_total = [], [], []
            for k in range(c):
                t = support_ref[r * slots + k]
                y = lane_block(y_ref, t)
                right = jnp.concatenate([y, y, pad_ones], axis=0)
                score = jnp.dot(left, right, preferred_element_type=F32).reshape(BLK // 8, 8, BLK)
                at = pl.ds(pl.multiple_of(jnp.where(k < live, t, tgt_blocks + k) * 8, 8), 8)
                own = jnp.max(score, axis=0)
                own_total = jnp.sum(jnp.exp2(score - own[None]), axis=0)
                old = high_ref[at, :]
                high = jnp.maximum(own, old)
                places.append(at)
                news_high.append(high)
                news_total.append(own_total * jnp.exp2(own - high) + total_ref[at, :] * jnp.exp2(old - high))
            for at, high, total in zip(places, news_high, news_total):
                high_ref[at, :] = high
                total_ref[at, :] = total

    by_group(counts_ref, order_ref, blocks, slots, work)

    def finish(step, _):
        at = [pl.ds(step * 64 + s, 8, stride=8) for s in range(8)]
        highs = [high_ref[a, :] for a in at]
        high = functools.reduce(jnp.maximum, highs)
        total = sum(total_ref[a, :] * jnp.exp2(h - high) for a, h in zip(at, highs))
        out_ref[pl.ds(pl.multiple_of(step * 8, 8), 8), :] = jnp.where(total > 0.0, high + jnp.log2(total), NEG)
        return 0

    lax.fori_loop(0, tgt_blocks // 8, finish, 0)


def exchange_kernel(axis, n, part_ref, out_ref, parts, whole, send_sem, recv_sem, send_sem2, recv_sem2):
    me = lax.axis_index(axis)
    rows = part_ref.shape[0] // n
    barrier = pltpu.get_barrier_semaphore()
    peers = [lax.rem(me + s, n) for s in range(1, n)]
    for peer in peers:
        pl.semaphore_signal(barrier, inc=1, device_id={axis: peer}, device_id_type=MESH)
    pl.semaphore_wait(barrier, n - 1)

    def chunk(i):
        return pl.ds(pl.multiple_of(i * rows, rows), rows)

    copies = []
    for s, peer in enumerate(peers):
        copy = pltpu.make_async_remote_copy(
            src_ref=part_ref.at[chunk(peer)],
            dst_ref=parts.at[s],
            send_sem=send_sem.at[s],
            recv_sem=recv_sem.at[s],
            device_id={axis: peer},
            device_id_type=MESH,
        )
        copy.start()
        copies.append(copy)
    mine = part_ref[chunk(me), :]
    for copy in copies:
        copy.wait()
    high = mine
    for s in range(n - 1):
        high = jnp.maximum(high, parts[s])
    total = jnp.exp2(mine - high)
    for s in range(n - 1):
        total = total + jnp.exp2(parts[s] - high)
    whole[chunk(me), :] = high + jnp.log2(total)
    copies = []
    for s, peer in enumerate(peers):
        copy = pltpu.make_async_remote_copy(
            src_ref=whole.at[chunk(me)],
            dst_ref=whole.at[chunk(me)],
            send_sem=send_sem2.at[s],
            recv_sem=recv_sem2.at[s],
            device_id={axis: peer},
            device_id_type=MESH,
        )
        copy.start()
        copies.append(copy)
    for copy in copies:
        copy.wait()
    out_ref[...] = whole[...]


def exchange(axis, n, cid, part):
    return pl.pallas_call(
        functools.partial(exchange_kernel, axis, n),
        out_shape=jax.ShapeDtypeStruct(part.shape, F32),
        in_specs=[pl.BlockSpec(memory_space=pltpu.VMEM)],
        out_specs=pl.BlockSpec(memory_space=pltpu.VMEM),
        scratch_shapes=[
            pltpu.VMEM((n - 1, part.shape[0] // n, BLK), F32),
            pltpu.VMEM(part.shape, F32),
            pltpu.SemaphoreType.DMA((n - 1,)),
            pltpu.SemaphoreType.DMA((n - 1,)),
            pltpu.SemaphoreType.DMA((n - 1,)),
            pltpu.SemaphoreType.DMA((n - 1,)),
        ],
        compiler_params=pltpu.CompilerParams(collective_id=cid, has_side_effects=True),
        name="exchange_" + axis,
    )(part)


VMEM = pl.BlockSpec(memory_space=pltpu.VMEM)
SMEM = pl.BlockSpec(memory_space=pltpu.SMEM)


def row_pass(support, counts, x, y, g):
    blocks, slots, tgt_blocks = counts.shape[0], support.shape[0] // counts.shape[0], g.shape[0]
    return pl.pallas_call(
        row_kernel,
        out_shape=jax.ShapeDtypeStruct((blocks, BLK), F32),
        in_specs=[SMEM, SMEM, VMEM, VMEM, VMEM],
        out_specs=VMEM,
        scratch_shapes=[
            pltpu.SMEM((blocks,), jnp.int32),
            pltpu.SMEM((slots + 2,), jnp.int32),
            pltpu.VMEM((tgt_blocks + 1, 16, BLK), BF16),
            pltpu.VMEM((GROUP * slots, BLK, BLK), F32),
        ],
        compiler_params=pltpu.CompilerParams(vmem_limit_bytes=48 * 2**20),
        name="row_pass",
    )(support, counts, x, y, g)


def col_pass(log_total, support, counts, x, y, lse):
    blocks, slots, tgt_blocks = counts.shape[0], support.shape[0] // counts.shape[0], y.shape[1] // BLK
    return pl.pallas_call(
        functools.partial(col_kernel, log_total),
        out_shape=(jax.ShapeDtypeStruct((blocks, BLK), F32), jax.ShapeDtypeStruct((tgt_blocks, BLK), F32)),
        in_specs=[SMEM, SMEM, VMEM, VMEM, VMEM],
        out_specs=(VMEM, VMEM),
        scratch_shapes=[
            pltpu.SMEM((blocks,), jnp.int32),
            pltpu.SMEM((slots + 2,), jnp.int32),
            pltpu.VMEM((tgt_blocks * 8 + 64, BLK), F32),
            pltpu.VMEM((tgt_blocks * 8 + 64, BLK), F32),
        ],
        compiler_params=pltpu.CompilerParams(vmem_limit_bytes=48 * 2**20),
        name="col_pass",
    )(support, counts, x, y, lse)


def body(src_points, tgt_points, tgt_potential, support, counts):
    features = src_points.shape[0]
    total_src = src_points.shape[1] * lax.axis_size("src")
    total_tgt = tgt_points.shape[1] * lax.axis_size("tgt")
    flat_support = support.reshape(-1)
    flat_counts = counts.reshape(-1)
    row_part = row_pass(flat_support, flat_counts, src_points, tgt_points, tgt_potential.reshape(-1, BLK))
    row_lse = exchange("tgt", lax.axis_size("tgt"), 0, row_part)
    src_potential, col_part = col_pass(math.log(total_tgt), flat_support, flat_counts, src_points, tgt_points, row_lse)
    col_lse = exchange("src", lax.axis_size("src"), 1, col_part)
    tgt_sq = jnp.sum(jnp.square(tgt_points.astype(F32)), axis=0)
    new_tgt = tgt_sq / (2 * features) - FROM_LOG2 * col_lse.reshape(-1) + BLUR * math.log(total_src)
    return src_potential.reshape(-1), new_tgt


def solution(mesh):
    return jax.shard_map(
        body,
        mesh=mesh,
        in_specs=(P(None, "src"), P(None, "tgt"), P("tgt"), P("src", "tgt", None), P("src", "tgt")),
        out_specs=(P("src"), P("tgt")),
        check_vma=False,
    )
```

time: 695 us -> 104 us (0.15)
  waiting for transfers between devices: 360 us -> 0 us
  local copies, waits for them, and re-layouts: 150 us -> 10.3 us
  Pallas kernels: 0 us -> 88.6 us
  matrix products: 76.1 us -> 0 us
  loops' own time: 45.3 us -> 0 us
  other arithmetic: 47.1 us -> 4.24 us
  between operations: 14 us -> 0.73 us
    psum x2 -> x0, waiting for transfers between devices: 184 us -> none  [the longest x1 113 us: body(): global_total = lax.psum(col_total * jnp.exp(col_high - global_high), 'src')]
    pmax x2 -> x0, waiting for transfers between devices: 175 us -> none  [the longest x1 106 us: body(): global_high = lax.pmax(col_high, 'src')]
    gather x128 -> x0, local copies, waits for them, and re-layouts: 118 us -> none  [the longest x32 90 us: group_cost(): jnp.take(tgt_cube, picked.reshape(-1), axis=1)]
    pallas_call x0 -> x4, Pallas kernels: none -> 88.6 us  [the longest x2 40.4 us: exchange(): pl.pallas_call(functools.partial(exchange_kernel, axis, n), out_shape=jax...]
    dot_general x32 -> x0, matrix products: 76.1 us -> none  [group_cost(): jnp.einsum('dgi,dgkj->gikj', src_rows, near_points, preferred_element_typ...]
    another operation x2 -> x0, loops' own time: 45.3 us -> none  [the longest x1 22.7 us: body(): lax.map(col_part, jnp.arange(step_count, dtype=jnp.int32))]
    dynamic_slice x112 -> x0, local copies, waits for them, and re-layouts: 19.6 us -> none  [the longest x32 18.8 us: body(): lax.map(row_part, jnp.arange(step_count, dtype=jnp.int32))]
    reduce_sum x34 -> x1, other arithmetic: 20 us -> 3.48 us  [body(): tgt_sq = jnp.sum(jnp.square(tgt_points.astype(F32)), axis=0)]
  transfers between devices with their start and end apart: 4 -> 0, of which waited for: 4 -> 0; matrix products, arithmetic and copies ran while one was open for 1% -> 0% of each run, Pallas kernels for 0% -> 0%
where the time goes in v1:
time: 104 us
  Pallas kernels  88.6 us (85%)
  local copies, waits for them, and re-layouts  10.3 us (10%)
  other arithmetic  4.24 us (4%)
    pallas_call x2, Pallas kernels, exchange(): pl.pallas_call(functools.partial(exchange_kernel, axis, n), out_shape=jax...  40.4 us
    pallas_call x1, Pallas kernels, row_pass(): pl.pallas_call(row_kernel, out_shape=jax.ShapeDtypeStruct((blocks, BLK),...  25.9 us
    pallas_call x1, Pallas kernels, col_pass(): pl.pallas_call(functools.partial(col_kernel, log_total), out_shape=(jax.S...  22.3 us
    unnamed x23, local copies, waits for them, and re-layouts  10.2 us
    reduce_sum x1, other arithmetic, body(): tgt_sq = jnp.sum(jnp.square(tgt_points.astype(F32)), axis=0)  3.48 us

profile of v1, /device:TPU:1, one launch (start us, length us, event | category | flops | bytes accessed | tf_op | source)
XLA Modules:
  0.0 103.9 jit_solution(13721253472164677467)
XLA Ops:
  0.6 0.0 copy-start.9
  0.6 0.8 copy.7
  1.4 0.1 reshape.19.support_ref
  1.6 0.0 copy-start
  1.6 2.2 %copy-done = bf16[32,65536]{1,0:T(8,128)(2,1)S(1)} copy-done((bf16[32,65536]{1,0:T(8,128)(2,1)S(1)}, bf16[32,65536]{1,0:T(8,128)(2,1)}, u32[]{:S(2)}) %copy-start) | copy-done | bytes 4194328
  3.8 0.0 copy-start.2
  3.8 1.2 %copy-done.2 = bf16[32,16384]{1,0:T(8,128)(2,1)S(1)} copy-done((bf16[32,16384]{1,0:T(8,128)(2,1)S(1)}, bf16[32,16384]{1,0:T(8,128)(2,1)}, u32[]{:S(2)}) %copy-start.2) | copy-done | bytes 1048600
  5.0 0.0 copy-start.6
  5.0 0.9 copy-done.6
  5.9 0.0 copy-start.8
  5.9 0.7 copy-done.8
  6.6 0.0 copy-start.3
  6.6 25.9 %row_pass.1.part_ref = f32[128,128]{1,0:T(8,128)S(1)} custom-call(s32[768]{0:T(1024)S(1)} %reshape.19.support_ref, s32[128]{0:T(128)S(1)} %bitcast.10, bf16[32,16384]{1,0:T(8,128)(2,1)S(1)} %copy-done.2, bf16[32,65536]{1,0:T(8,128)(2,1)S(1)} %copy-done, f32[512,128]{1,0:T(8,128)S(1)} %bitcast.9), custom_call_target="tpu_custom_call" | custom-call | tf_op jit(solution)/shard_map/row_pass/pallas_call | solution.py:263
  32.6 0.0 copy-start.5
  32.6 0.6 copy-done.5
  33.2 18.4 %exchange_tgt.1.lse_ref = f32[128,128]{1,0:T(8,128)} custom-call(f32[128,128]{1,0:T(8,128)} %copy-done.5), custom_call_target="tpu_custom_call" | custom-call | tf_op jit(solution)/shard_map/exchange_tgt/pallas_call | solution.py:239
  51.6 0.0 copy-done.9
  51.6 0.0 copy-done.3
  51.7 0.0 copy-start.1
  51.7 2.2 %copy-done.1 = bf16[32,65536]{1,0:T(8,128)(2,1)S(1)} copy-done((bf16[32,65536]{1,0:T(8,128)(2,1)S(1)}, bf16[32,65536]{1,0:T(8,128)(2,1)}, u32[]{:S(2)}) %copy-start.1) | copy-done | bytes 4194328
  53.8 0.0 copy-start.4
  53.8 0.8 copy-done.4
  54.7 22.3 %col_pass.1 = (f32[128,128]{1,0:T(8,128)}, f32[512,128]{1,0:T(8,128)S(1)}) custom-call(s32[768]{0:T(1024)S(1)} %reshape.19.support_ref, s32[128]{0:T(128)S(1)} %bitcast.11, bf16[32,16384]{1,0:T(8,128)(2,1)S(1)} %copy-done.3, bf16[32,65536]{1,0:T(8,128)(2,1)S(1)} %copy-done.1, f32[128,128]{1,0:T(8,128)S(1)} %copy-done.4), custom_call_target="tpu_custom_call" | custom-call | tf_op jit(solution)/shard_map/col_pass/pallas_call | solution.py:281
  76.9 0.0 copy-start.7
  77.0 0.7 copy-done.7
  77.7 21.9 %exchange_src.1 = f32[512,128]{1,0:T(8,128)} custom-call(f32[512,128]{1,0:T(8,128)} %copy-done.7), custom_call_target="tpu_custom_call" | custom-call | tf_op jit(solution)/shard_map/exchange_src/pallas_call | solution.py:239
  99.6 0.0 copy-start.10
  99.6 3.5 %multiply_reduce_fusion = f32[65536]{0:T(1024)S(1)} fusion(bf16[32,65536]{1,0:T(8,128)(2,1)} %y_ref.3), kind=kLoop, calls=%fused_computation | loop fusion | flops 6225920 | bytes 4456448 | tf_op jit(solution)/shard_map/reduce_sum | solution.py:307
  103.1 0.0 copy-done.10
  103.1 0.8 fusion
Async XLA Ops:
  0.6 51.0 %copy-start.9 = (s32[128,1]{0,1:T(1,128)S(1)}, s32[128,1]{0,1:T(1,128)}, u32[]{:S(2)}) copy-start(s32[128,1]{0,1:T(1,128)} %param.9) | copy-start | bytes 1540
  1.6 2.2 %copy-start = (bf16[32,65536]{1,0:T(8,128)(2,1)S(1)}, bf16[32,65536]{1,0:T(8,128)(2,1)}, u32[]{:S(2)}) copy-start(bf16[32,65536]{1,0:T(8,128)(2,1)} %y_ref.3) | copy-start | bytes 12582916
  3.8 1.2 %copy-start.2 = (bf16[32,16384]{1,0:T(8,128)(2,1)S(1)}, bf16[32,16384]{1,0:T(8,128)(2,1)}, u32[]{:S(2)}) copy-start(bf16[32,16384]{1,0:T(8,128)(2,1)} %x_ref.3) | copy-start | bytes 3145732
  5.0 0.9 copy-start.6
  5.9 0.7 copy-start.8
  6.6 45.0 %copy-start.3 = (bf16[32,16384]{1,0:T(8,128)(2,1)S(1)}, bf16[32,16384]{1,0:T(8,128)(2,1)}, u32[]{:S(2)}) copy-start(bf16[32,16384]{1,0:T(8,128)(2,1)} %x_ref.3) | copy-start | bytes 3145732
  32.6 0.6 copy-start.5
  51.7 2.2 %copy-start.1 = (bf16[32,65536]{1,0:T(8,128)(2,1)S(1)}, bf16[32,65536]{1,0:T(8,128)(2,1)}, u32[]{:S(2)}) copy-start(bf16[32,65536]{1,0:T(8,128)(2,1)} %y_ref.3) | copy-start | bytes 12582916
  53.8 0.8 copy-start.4
  76.9 0.7 copy-start.7
  99.6 3.5 %copy-start.10 = (f32[512,128]{1,0:T(8,128)S(1)}, f32[512,128]{1,0:T(8,128)}, u32[]{:S(2)}) copy-start(f32[512,128]{1,0:T(8,128)} %exchange_src.1) | copy-start | bytes 786436

commit v2 on v1

v2 whole, which is shorter than its diff:
```python
import functools
import math

import jax
import jax.numpy as jnp
from jax import lax
from jax.experimental import pallas as pl
from jax.experimental.pallas import tpu as pltpu
from jax.sharding import PartitionSpec as P

BLK = 128
BLUR = 0.05
NEG = -1e30
TO_LOG2 = math.log2(math.e) / BLUR
FROM_LOG2 = BLUR * math.log(2.0)
GROUP = 32
F32 = jnp.float32
BF16 = jnp.bfloat16
MESH = pl.DeviceIdType.MESH


def three_parts(v):
    hi = v.astype(BF16).astype(F32)
    mid = (v - hi).astype(BF16).astype(F32)
    return hi, mid, v - hi - mid


def split_source(x, scale):
    scaled = x.astype(F32) * scale
    hi = scaled.astype(BF16)
    return hi, (scaled - hi.astype(F32)).astype(BF16)


def list_tiles(support_ref, counts_ref, list_ref, blocks, slots):
    def place(r, at):
        for k in range(slots):
            list_ref[at + k] = support_ref[k * blocks + r] * (8 * blocks) + (r * 8 + k)
        return at + counts_ref[r]

    live = lax.fori_loop(0, blocks, place, 0)
    for q in range(2 * GROUP):
        list_ref[live + q] = 7
    return (live + (GROUP - 1)) // GROUP


def lane_block(ref, index):
    return ref[:, pl.ds(pl.multiple_of(index * BLK, BLK), BLK)]


def eight_rows(index):
    return pl.ds(pl.multiple_of(index * 8, 8), 8)


def tile_score(left, right):
    return lax.dot_general(left, right, (((0,), (0,)), ((), ())), preferred_element_type=F32)


def tile_sums(score):
    score = score.reshape(BLK // 8, 8, BLK)
    high = jnp.max(score, axis=0)
    return high, jnp.sum(jnp.exp2(score - high[None]), axis=0)


def pipeline(list_ref, steps, score_ref, begin, end):
    for q in range(GROUP):
        score_ref[q] = begin(list_ref[q])

    def step(i, _):
        for q in range(GROUP):
            end(list_ref[i * GROUP + q], score_ref[q])
            score_ref[q] = begin(list_ref[(i + 1) * GROUP + q])
        return 0

    lax.fori_loop(0, steps, step, 0)


def merged_rows(high_ref, total_ref, step, stride):
    at = [pl.ds(step * 8 * stride + s, 8, stride=stride) for s in range(8)]
    highs = [high_ref[a, :] for a in at]
    high = functools.reduce(jnp.maximum, highs)
    total = sum(total_ref[a, :] * jnp.exp2(h - high) for a, h in zip(at, highs))
    return jnp.where(total > 0.0, high + jnp.log2(total), NEG)


def row_kernel(support_ref, counts_ref, x_any, y_any, g_any, out_ref, list_ref, x_ref, y_ref, g_ref, right_ref, high_ref, total_ref, score_ref, sem):
    blocks = out_ref.shape[0]
    slots = support_ref.shape[0] // blocks
    features = x_ref.shape[0]
    copies = [pltpu.make_async_copy(a, b, sem.at[i]) for i, (a, b) in enumerate(((x_any, x_ref), (y_any, y_ref), (g_any, g_ref)))]
    for copy in copies:
        copy.start()
    steps = list_tiles(support_ref, counts_ref, list_ref, blocks, slots)

    def clear(step, _):
        at = pl.ds(pl.multiple_of(step * 64, 64), 64)
        high_ref[at, :] = jnp.full((64, BLK), NEG, F32)
        total_ref[at, :] = jnp.zeros((64, BLK), F32)
        return 0

    lax.fori_loop(0, blocks, clear, 0)
    copies[0].wait()
    ones = jnp.where(lax.broadcasted_iota(jnp.int32, (32, BLK), 0) < 24, 1.0, 0.0).astype(BF16)

    def prepare(r, _):
        hi, lo = split_source(lane_block(x_ref, r), TO_LOG2 / features)
        right_ref[r] = jnp.concatenate([hi, lo, ones], axis=0)
        return 0

    lax.fori_loop(0, blocks, prepare, 0, unroll=4)
    copies[1].wait()
    copies[2].wait()

    slot_bits = (8 * blocks).bit_length() - 1

    def begin(code):
        t = lax.shift_right_logical(code, slot_bits)
        r = lax.shift_right_logical(jnp.bitwise_and(code, 8 * blocks - 1), 3)
        y = lane_block(y_ref, t)
        yf = y.astype(F32)
        sq = yf * yf
        sq = functools.reduce(jnp.add, [sq[i : i + 8] for i in range(0, features, 8)])
        bias = (TO_LOG2 / 8) * g_ref[pl.ds(t, 1), :] - (TO_LOG2 / (2 * features)) * sq
        hi, mid, lo = three_parts(bias)
        extra = jnp.concatenate([hi, mid, lo, jnp.zeros((8, BLK), F32)], axis=0).astype(BF16)
        return tile_score(jnp.concatenate([y, y, extra], axis=0), right_ref[r])

    def end(code, score):
        slot = jnp.bitwise_and(code, 8 * blocks - 1)
        high, total = tile_sums(score)
        high_ref[eight_rows(slot), :] = high
        total_ref[eight_rows(slot), :] = total

    pipeline(list_ref, steps, score_ref, begin, end)

    def merge(step, _):
        for q in range(8):
            r = step * 8 + q
            highs = [high_ref[eight_rows(r * 8 + k), :] for k in range(slots)]
            high = functools.reduce(jnp.maximum, highs)
            total = sum(total_ref[eight_rows(r * 8 + k), :] * jnp.exp2(h - high) for k, h in enumerate(highs))
            high_ref[eight_rows(r * 8), :] = high
            total_ref[eight_rows(r * 8), :] = total
        out_ref[eight_rows(step), :] = merged_rows(high_ref, total_ref, step, 64)
        return 0

    lax.fori_loop(0, blocks // 8, merge, 0)


def col_kernel(log_total, support_ref, counts_ref, x_ref, y_ref, lse_ref, pot_ref, out_any, list_ref, out_ref, left_ref, high_ref, total_ref, score_ref, sem):
    blocks = pot_ref.shape[0]
    slots = support_ref.shape[0] // blocks
    features = x_ref.shape[0]
    tgt_blocks = out_ref.shape[0]
    steps = list_tiles(support_ref, counts_ref, list_ref, blocks, slots)

    def clear(step, _):
        at = pl.ds(pl.multiple_of(step * 64, 64), 64)
        high_ref[at, :] = jnp.full((64, BLK), NEG, F32)
        total_ref[at, :] = jnp.zeros((64, BLK), F32)
        return 0

    lax.fori_loop(0, high_ref.shape[0] // 64, clear, 0)
    sub = lax.broadcasted_iota(jnp.int32, (16, BLK), 0)
    ones = jnp.where(sub < 3, 1.0, 0.0).astype(BF16)

    def prepare(r, _):
        x = lane_block(x_ref, r)
        xf = x.astype(F32)
        pot = -FROM_LOG2 * lse_ref[pl.ds(r, 1), :] + BLUR * log_total
        pot_ref[pl.ds(r, 1), :] = pot + jnp.sum(xf * xf, axis=0, keepdims=True) * (1.0 / (2 * features))
        hi, mid, lo = three_parts(TO_LOG2 * pot)
        extra = jnp.where(sub == 0, hi, jnp.where(sub == 1, mid, jnp.where(sub == 2, lo, 0.0))).astype(BF16)
        left_ref[r] = jnp.concatenate([*split_source(x, TO_LOG2 / features), extra], axis=0)
        return 0

    lax.fori_loop(0, blocks, prepare, 0, unroll=4)

    slot_bits = (8 * blocks).bit_length() - 1

    def begin(code):
        y = lane_block(y_ref, lax.shift_right_logical(code, slot_bits))
        r = lax.shift_right_logical(jnp.bitwise_and(code, 8 * blocks - 1), 3)
        return tile_score(left_ref[r], jnp.concatenate([y, y, ones], axis=0))

    def end(code, score):
        t = lax.shift_right_logical(code, slot_bits)
        own, own_total = tile_sums(score)
        at = eight_rows(jnp.where(jnp.bitwise_and(code, 7) == 7, tgt_blocks, t))
        old = high_ref[at, :]
        high = jnp.maximum(own, old)
        high_ref[at, :] = high
        total_ref[at, :] = own_total * jnp.exp2(own - high) + total_ref[at, :] * jnp.exp2(old - high)

    pipeline(list_ref, steps, score_ref, begin, end)

    def finish(step, _):
        out_ref[eight_rows(step), :] = merged_rows(high_ref, total_ref, step, 8)
        return 0

    pieces = 4
    size = tgt_blocks // pieces
    copies = []
    for piece in range(pieces):
        lax.fori_loop(piece * size // 8, (piece + 1) * size // 8, finish, 0, unroll=2)
        rows = pl.ds(piece * size, size)
        copies.append(pltpu.make_async_copy(out_ref.at[rows], out_any.at[rows], sem.at[piece]))
        copies[-1].start()
    for copy in copies:
        copy.wait()


def exchange_kernel(axis, n, shift, part_any, y_any, out_ref, mine_ref, parts, whole, y_ref, sq_ref, local_sem, send_sem, recv_sem, send_sem2, recv_sem2):
    me = lax.axis_index(axis)
    rows = part_any.shape[0] // n

    def chunk(i):
        return pl.ds(pl.multiple_of(i * rows, rows), rows)

    mine_copy = pltpu.make_async_copy(part_any.at[chunk(me)], mine_ref, local_sem.at[0])
    mine_copy.start()
    barrier = pltpu.get_barrier_semaphore()
    peers = [lax.rem(me + s, n) for s in range(1, n)]
    for peer in peers:
        pl.semaphore_signal(barrier, inc=1, device_id={axis: peer}, device_id_type=MESH)
    if y_any is not None:
        width = rows * BLK
        y_copy = pltpu.make_async_copy(y_any.at[:, pl.ds(pl.multiple_of(me * width, width), width)], y_ref, local_sem.at[1])
        y_copy.start()
        y_copy.wait()
        y = y_ref[...].astype(F32)
        sq = jnp.sum(y * y, axis=0, keepdims=True) * (1.0 / (2 * y.shape[0]))
        for q in range(rows):
            sq_ref[pl.ds(q, 1), :] = sq[:, q * BLK : (q + 1) * BLK]
    mine_copy.wait()
    pl.semaphore_wait(barrier, n - 1)

    copies = []
    for s, peer in enumerate(peers):
        copy = pltpu.make_async_remote_copy(
            src_ref=part_any.at[chunk(peer)],
            dst_ref=parts.at[s],
            send_sem=send_sem.at[s],
            recv_sem=recv_sem.at[s],
            device_id={axis: peer},
            device_id_type=MESH,
        )
        copy.start()
        copies.append(copy)
    mine = mine_ref[...]
    for copy in copies:
        copy.wait()
    high = mine
    for s in range(n - 1):
        high = jnp.maximum(high, parts[s])
    total = jnp.exp2(mine - high)
    for s in range(n - 1):
        total = total + jnp.exp2(parts[s] - high)
    result = high + jnp.log2(total)
    if y_any is not None:
        result = sq_ref[...] - FROM_LOG2 * result + shift
    whole[chunk(me), :] = result
    copies = []
    for s, peer in enumerate(peers):
        copy = pltpu.make_async_remote_copy(
            src_ref=whole.at[chunk(me)],
            dst_ref=whole.at[chunk(me)],
            send_sem=send_sem2.at[s],
            recv_sem=recv_sem2.at[s],
            device_id={axis: peer},
            device_id_type=MESH,
        )
        copy.start()
        copies.append(copy)
    for copy in copies:
        copy.wait()
    out_ref[...] = whole[...]


def row_exchange_kernel(axis, n, part_any, out_ref, *scratch):
    exchange_kernel(axis, n, 0.0, part_any, None, out_ref, *scratch[:3], None, None, *scratch[3:])


def exchange(axis, n, cid, shift, part, y=None):
    rows = part.shape[0] // n
    extra = [] if y is None else [pltpu.VMEM((y.shape[0], rows * BLK), BF16), pltpu.VMEM((rows, BLK), F32)]
    kernel = functools.partial(row_exchange_kernel, axis, n) if y is None else functools.partial(exchange_kernel, axis, n, shift)
    operands = (part,) if y is None else (part, y)
    return pl.pallas_call(
        kernel,
        out_shape=jax.ShapeDtypeStruct(part.shape, F32),
        in_specs=[pl.BlockSpec(memory_space=pl.ANY)] * len(operands),
        out_specs=pl.BlockSpec(memory_space=pltpu.VMEM),
        scratch_shapes=[
            pltpu.VMEM((rows, BLK), F32),
            pltpu.VMEM((n - 1, rows, BLK), F32),
            pltpu.VMEM(part.shape, F32),
            *extra,
            pltpu.SemaphoreType.DMA((2,)),
            pltpu.SemaphoreType.DMA((n - 1,)),
            pltpu.SemaphoreType.DMA((n - 1,)),
            pltpu.SemaphoreType.DMA((n - 1,)),
            pltpu.SemaphoreType.DMA((n - 1,)),
        ],
        compiler_params=pltpu.CompilerParams(collective_id=cid, has_side_effects=True, vmem_limit_bytes=8 * 2**20),
        name="exchange_" + axis,
    )(*operands)


VMEM = pl.BlockSpec(memory_space=pltpu.VMEM)
SMEM = pl.BlockSpec(memory_space=pltpu.SMEM)
ANY = pl.BlockSpec(memory_space=pl.ANY)


def row_pass(support, counts, x, y, g):
    blocks, slots = counts.shape[0], support.shape[0] // counts.shape[0]
    return pl.pallas_call(
        row_kernel,
        out_shape=jax.ShapeDtypeStruct((blocks, BLK), F32),
        in_specs=[SMEM, SMEM, ANY, ANY, ANY],
        out_specs=VMEM,
        scratch_shapes=[
            pltpu.SMEM((blocks * slots + 2 * GROUP + 8,), jnp.int32),
            pltpu.VMEM(x.shape, BF16),
            pltpu.VMEM(y.shape, BF16),
            pltpu.VMEM(g.shape, F32),
            pltpu.VMEM((blocks, 2 * x.shape[0] + 32, BLK), BF16),
            pltpu.VMEM((blocks * 64, BLK), F32),
            pltpu.VMEM((blocks * 64, BLK), F32),
            pltpu.VMEM((GROUP, BLK, BLK), F32),
            pltpu.SemaphoreType.DMA((3,)),
        ],
        name="row_pass",
        compiler_params=pltpu.CompilerParams(vmem_limit_bytes=56 * 2**20),
    )(support, counts, x, y, g)


def col_pass(log_total, support, counts, x, y, lse):
    blocks, slots, tgt_blocks = counts.shape[0], support.shape[0] // counts.shape[0], y.shape[1] // BLK
    return pl.pallas_call(
        functools.partial(col_kernel, log_total),
        out_shape=(jax.ShapeDtypeStruct((blocks, BLK), F32), jax.ShapeDtypeStruct((tgt_blocks, BLK), F32)),
        in_specs=[SMEM, SMEM, VMEM, VMEM, VMEM],
        out_specs=(VMEM, ANY),
        scratch_shapes=[
            pltpu.SMEM((blocks * slots + 2 * GROUP + 8,), jnp.int32),
            pltpu.VMEM((tgt_blocks, BLK), F32),
            pltpu.VMEM((blocks, 2 * x.shape[0] + 16, BLK), BF16),
            pltpu.VMEM((tgt_blocks * 8 + 64, BLK), F32),
            pltpu.VMEM((tgt_blocks * 8 + 64, BLK), F32),
            pltpu.VMEM((GROUP, BLK, BLK), F32),
            pltpu.SemaphoreType.DMA((4,)),
        ],
        name="col_pass",
        compiler_params=pltpu.CompilerParams(vmem_limit_bytes=40 * 2**20),
    )(support, counts, x, y, lse)


def body(src_points, tgt_points, tgt_potential, support, counts):
    total_src = src_points.shape[1] * lax.axis_size("src")
    total_tgt = tgt_points.shape[1] * lax.axis_size("tgt")
    flat_support = support.transpose(2, 1, 0).reshape(-1)
    flat_counts = counts.reshape(-1)
    row_part = row_pass(flat_support, flat_counts, src_points, tgt_points, tgt_potential.reshape(-1, BLK))
    row_lse = exchange("tgt", lax.axis_size("tgt"), 0, 0.0, row_part)
    src_potential, col_part = col_pass(math.log(total_tgt), flat_support, flat_counts, src_points, tgt_points, row_lse)
    new_tgt = exchange("src", lax.axis_size("src"), 1, BLUR * math.log(total_src), col_part, tgt_points)
    return src_potential.reshape(-1), new_tgt.reshape(-1)


def solution(mesh):
    return jax.shard_map(
        body,
        mesh=mesh,
        in_specs=(P(None, "src"), P(None, "tgt"), P("tgt"), P("src", "tgt", None), P("src", "tgt")),
        out_specs=(P("src"), P("tgt")),
        check_vma=False,
    )
```

time: 104 us -> 73.5 us (0.71)
  Pallas kernels: 88.6 us -> 69.8 us
  local copies, waits for them, and re-layouts: 10.3 us -> 2.83 us
  other arithmetic: 4.24 us -> 0 us
    pallas_call x1, Pallas kernels: 25.9 us -> 15.1 us  [row_pass(): pl.pallas_call(row_kernel, out_shape=jax.ShapeDtypeStruct((blocks, BLK),...]
    unnamed x23 -> x13, local copies, waits for them, and re-layouts: 10.2 us -> 2.22 us
    pallas_call x1, Pallas kernels: 22.3 us -> 15.3 us  [col_pass(): pl.pallas_call(functools.partial(col_kernel, log_total), out_shape=(jax.S...]
    reduce_sum x1 -> x0, other arithmetic: 3.48 us -> none  [body(): tgt_sq = jnp.sum(jnp.square(tgt_points.astype(F32)), axis=0)]
where the time goes in v2:
time: 73.5 us; the launch traced here: 73.4 us
  Pallas kernels  69.8 us (95%)
  local copies, waits for them, and re-layouts  2.83 us (4%)
    pallas_call x2, Pallas kernels, exchange(): pl.pallas_call(kernel, out_shape=jax.ShapeDtypeStruct(part.shape, F32), i...  39.4 us
    pallas_call x1, Pallas kernels, col_pass(): pl.pallas_call(functools.partial(col_kernel, log_total), out_shape=(jax.S...  15.3 us
    pallas_call x1, Pallas kernels, row_pass(): pl.pallas_call(row_kernel, out_shape=jax.ShapeDtypeStruct((blocks, BLK),...  15.1 us
    unnamed x13, local copies, waits for them, and re-layouts  2.22 us

profile of v2, /device:TPU:1, one launch (start us, length us, event | category | flops | bytes accessed | tf_op | source)
XLA Modules:
  0.0 73.4 jit_solution(16693037319026185077)
XLA Ops:
  0.6 0.0 copy-start
  0.6 0.0 copy-start.1
  0.7 0.0 copy-start.2
  0.7 0.0 copy-start.5
  0.7 0.6 copy-done
  1.3 0.6 bitcast_reduce_fusion
  1.9 0.0 copy-start.4
  1.9 15.1 %row_pass.1.part_any = f32[128,128]{1,0:T(8,128)} custom-call(s32[768]{0:T(1024)} %bitcast.8, s32[128]{0:T(128)} %bitcast.10, bf16[32,16384]{1,0:T(8,128)(2,1)} %x_ref.1, bf16[32,65536]{1,0:T(8,128)(2,1)} %y_any.3, f32[512,128]{1,0:T(8,128)} %bitcast.12), custom_call_target="tpu_custom_call" | custom-call | tf_op jit(solution)/shard_map/row_pass/pallas_call | solution.py:316
  17.1 0.0 copy-start.3
  17.1 0.8 %copy-done.3 = f32[128,128]{1,0:T(8,128)S(1)} copy-done((f32[128,128]{1,0:T(8,128)S(1)}, f32[128,128]{1,0:T(8,128)}, u32[]{:S(2)}) %copy-start.3) | copy-done | bytes 65560
  17.9 17.0 %exchange_tgt.1.lse_ref = f32[128,128]{1,0:T(8,128)S(1)} custom-call(f32[128,128]{1,0:T(8,128)S(1)} %copy-done.3), custom_call_target="tpu_custom_call" | custom-call | tf_op jit(solution)/shard_map/exchange_tgt/pallas_call | solution.py:288
  34.9 0.0 copy-done.1
  34.9 0.0 copy-done.2
  34.9 0.0 copy-done.5
  34.9 0.0 copy-done.4
  34.9 15.3 %col_pass.1 = (f32[128,128]{1,0:T(8,128)}, f32[512,128]{1,0:T(8,128)S(1)}) custom-call(s32[768]{0:T(1024)S(1)} %bitcast.9, s32[128]{0:T(128)S(1)} %bitcast.11, bf16[32,16384]{1,0:T(8,128)(2,1)S(1)} %copy-done.2, bf16[32,65536]{1,0:T(8,128)(2,1)S(1)} %copy-done.1, f32[128,128]{1,0:T(8,128)S(1)} %exchange_tgt.1.lse_ref), custom_call_target="tpu_custom_call" | custom-call | tf_op jit(solution)/shard_map/col_pass/pallas_call | solution.py:339
  50.2 22.4 %exchange_src.1 = f32[512,128]{1,0:T(8,128)S(1)} custom-call(f32[512,128]{1,0:T(8,128)S(1)} %get-tuple-element.5.part_any, bf16[32,65536]{1,0:T(8,128)(2,1)S(1)} %copy-done.1), custom_call_target="tpu_custom_call" | custom-call | tf_op jit(solution)/shard_map/exchange_src/pallas_call | solution.py:288
  72.7 0.7 copy.8
Async XLA Ops:
  0.6 0.7 copy-start
  0.6 34.3 %copy-start.1 = (bf16[32,65536]{1,0:T(8,128)(2,1)S(1)}, bf16[32,65536]{1,0:T(8,128)(2,1)}, u32[]{:S(2)}) copy-start(bf16[32,65536]{1,0:T(8,128)(2,1)} %y_any.3) | copy-start | bytes 12582916
  0.7 34.3 %copy-start.2 = (bf16[32,16384]{1,0:T(8,128)(2,1)S(1)}, bf16[32,16384]{1,0:T(8,128)(2,1)}, u32[]{:S(2)}) copy-start(bf16[32,16384]{1,0:T(8,128)(2,1)} %x_ref.1) | copy-start | bytes 3145732
  0.7 34.3 %copy-start.5 = (s32[128,1]{0,1:T(1,128)S(1)}, s32[128,1]{0,1:T(1,128)}, u32[]{:S(2)}) copy-start(s32[128,1]{0,1:T(1,128)} %param.9) | copy-start | bytes 1540
  1.9 33.0 %copy-start.4 = (s32[6,128]{1,0:T(8,128)S(1)}, s32[6,128]{1,0:T(8,128)}, u32[]{:S(2)}) copy-start(s32[6,128]{1,0:T(8,128)} %bitcast_reduce_fusion) | copy-start | bytes 9220
  17.1 0.8 %copy-start.3 = (f32[128,128]{1,0:T(8,128)S(1)}, f32[128,128]{1,0:T(8,128)}, u32[]{:S(2)}) copy-start(f32[128,128]{1,0:T(8,128)} %row_pass.1.part_any) | copy-start | bytes 196612

commit v3 on v2

v3 whole, which is shorter than its diff:
```python
import functools
import math

import jax
import jax.numpy as jnp
from jax import lax
from jax.experimental import pallas as pl
from jax.experimental.pallas import tpu as pltpu
from jax.sharding import PartitionSpec as P

BLK = 128
BLUR = 0.05
NEG = -1e30
TO_LOG2 = math.log2(math.e) / BLUR
FROM_LOG2 = BLUR * math.log(2.0)
GROUP = 32
F32 = jnp.float32
BF16 = jnp.bfloat16
MESH = pl.DeviceIdType.MESH


def three_parts(v):
    hi = v.astype(BF16).astype(F32)
    mid = (v - hi).astype(BF16).astype(F32)
    return hi, mid, v - hi - mid


def split_source(x, scale):
    scaled = x.astype(F32) * scale
    hi = scaled.astype(BF16)
    return hi, (scaled - hi.astype(F32)).astype(BF16)


def list_tiles(support_ref, counts_ref, list_ref, blocks, slots):
    def place(r, at):
        for k in range(slots):
            list_ref[at + k] = support_ref[k, 0, r] * (8 * blocks) + (r * 8 + k)
        return at + counts_ref[r]

    live = lax.fori_loop(0, blocks, place, 0)
    for q in range(2 * GROUP):
        list_ref[live + q] = 7
    list_ref[list_ref.shape[0] - 1] = (live + (GROUP - 1)) // GROUP


def lane_block(ref, index):
    return ref[:, pl.ds(pl.multiple_of(index * BLK, BLK), BLK)]


def eight_rows(index):
    return pl.ds(pl.multiple_of(index * 8, 8), 8)


def tile_score(left, right):
    return lax.dot_general(left, right, (((0,), (0,)), ((), ())), preferred_element_type=F32)


def tile_sums(score):
    score = score.reshape(BLK // 8, 8, BLK)
    high = jnp.max(score, axis=0)
    return high, jnp.sum(jnp.exp2(score - high[None]), axis=0)


def pipeline(list_ref, score_ref, begin, end):
    for q in range(GROUP):
        score_ref[q] = begin(list_ref[q])

    def step(i, _):
        for q in range(GROUP):
            end(list_ref[i * GROUP + q], score_ref[q])
            score_ref[q] = begin(list_ref[(i + 1) * GROUP + q])
        return 0

    lax.fori_loop(0, list_ref[list_ref.shape[0] - 1], step, 0)


def merged_rows(high_ref, total_ref, step, stride):
    at = [pl.ds(step * 8 * stride + s, 8, stride=stride) for s in range(8)]
    highs = [high_ref[a, :] for a in at]
    high = functools.reduce(jnp.maximum, highs)
    total = sum(total_ref[a, :] * jnp.exp2(h - high) for a, h in zip(at, highs))
    return jnp.where(total > 0.0, high + jnp.log2(total), NEG)


def row_kernel(support_any, counts_any, x_any, y_any, g_any, out_ref, list_any, support_ref, counts_ref, list_ref, x_ref, y_ref, g_ref, right_ref, high_ref, total_ref, score_ref, sem):
    blocks = out_ref.shape[0]
    slots = support_ref.shape[0]
    features = x_ref.shape[0]
    pairs = ((support_any, support_ref), (counts_any, counts_ref), (x_any, x_ref), (y_any, y_ref), (g_any, g_ref))
    copies = [pltpu.make_async_copy(a, b, sem.at[i]) for i, (a, b) in enumerate(pairs)]
    for copy in copies:
        copy.start()
    copies[0].wait()
    copies[1].wait()
    list_tiles(support_ref, counts_ref, list_ref, blocks, slots)
    list_copy = pltpu.make_async_copy(list_ref, list_any, sem.at[5])
    list_copy.start()

    def clear(step, _):
        at = pl.ds(pl.multiple_of(step * 64, 64), 64)
        high_ref[at, :] = jnp.full((64, BLK), NEG, F32)
        total_ref[at, :] = jnp.zeros((64, BLK), F32)
        return 0

    lax.fori_loop(0, blocks, clear, 0)
    copies[2].wait()
    ones = jnp.where(lax.broadcasted_iota(jnp.int32, (32, BLK), 0) < 24, 1.0, 0.0).astype(BF16)

    def prepare(r, _):
        hi, lo = split_source(lane_block(x_ref, r), TO_LOG2 / features)
        right_ref[r] = jnp.concatenate([hi, lo, ones], axis=0)
        return 0

    lax.fori_loop(0, blocks, prepare, 0, unroll=16)
    copies[3].wait()
    copies[4].wait()

    slot_bits = (8 * blocks).bit_length() - 1

    def begin(code):
        t = lax.shift_right_logical(code, slot_bits)
        r = lax.shift_right_logical(jnp.bitwise_and(code, 8 * blocks - 1), 3)
        y = lane_block(y_ref, t)
        yf = y.astype(F32)
        sq = yf * yf
        sq = functools.reduce(jnp.add, [sq[i : i + 8] for i in range(0, features, 8)])
        bias = (TO_LOG2 / 8) * g_ref[pl.ds(t, 1), :] - (TO_LOG2 / (2 * features)) * sq
        hi, mid, lo = three_parts(bias)
        extra = jnp.concatenate([hi, mid, lo, jnp.zeros((8, BLK), F32)], axis=0).astype(BF16)
        return tile_score(jnp.concatenate([y, y, extra], axis=0), right_ref[r])

    def end(code, score):
        slot = jnp.bitwise_and(code, 8 * blocks - 1)
        high, total = tile_sums(score)
        high_ref[eight_rows(slot), :] = high
        total_ref[eight_rows(slot), :] = total

    pipeline(list_ref, score_ref, begin, end)

    def merge(step, _):
        for q in range(8):
            r = step * 8 + q
            highs = [high_ref[eight_rows(r * 8 + k), :] for k in range(slots)]
            high = functools.reduce(jnp.maximum, highs)
            total = sum(total_ref[eight_rows(r * 8 + k), :] * jnp.exp2(h - high) for k, h in enumerate(highs))
            high_ref[eight_rows(r * 8), :] = high
            total_ref[eight_rows(r * 8), :] = total
        out_ref[eight_rows(step), :] = merged_rows(high_ref, total_ref, step, 64)
        return 0

    lax.fori_loop(0, blocks // 8, merge, 0, unroll=4)
    list_copy.wait()


def col_kernel(log_total, list_any, x_ref, y_ref, lse_ref, pot_any, out_any, list_ref, pot_ref, out_ref, left_ref, high_ref, total_ref, score_ref, sem):
    blocks = pot_ref.shape[0]
    features = x_ref.shape[0]
    tgt_blocks = out_ref.shape[0]

    list_copy = pltpu.make_async_copy(list_any, list_ref, sem.at[4])
    list_copy.start()

    def clear(step, _):
        at = pl.ds(pl.multiple_of(step * 64, 64), 64)
        high_ref[at, :] = jnp.full((64, BLK), NEG, F32)
        total_ref[at, :] = jnp.zeros((64, BLK), F32)
        return 0

    lax.fori_loop(0, high_ref.shape[0] // 64, clear, 0)
    sub = lax.broadcasted_iota(jnp.int32, (16, BLK), 0)
    ones = jnp.where(sub < 3, 1.0, 0.0).astype(BF16)

    def prepare(r, _):
        x = lane_block(x_ref, r)
        xf = x.astype(F32)
        pot = -FROM_LOG2 * lse_ref[pl.ds(r, 1), :] + BLUR * log_total
        pot_ref[pl.ds(r, 1), :] = pot + jnp.sum(xf * xf, axis=0, keepdims=True) * (1.0 / (2 * features))
        hi, mid, lo = three_parts(TO_LOG2 * pot)
        extra = jnp.where(sub == 0, hi, jnp.where(sub == 1, mid, jnp.where(sub == 2, lo, 0.0))).astype(BF16)
        left_ref[r] = jnp.concatenate([*split_source(x, TO_LOG2 / features), extra], axis=0)
        return 0

    lax.fori_loop(0, blocks, prepare, 0, unroll=16)
    pot_copy = pltpu.make_async_copy(pot_ref, pot_any, sem.at[5])
    pot_copy.start()
    list_copy.wait()

    slot_bits = (8 * blocks).bit_length() - 1

    def begin(code):
        y = lane_block(y_ref, lax.shift_right_logical(code, slot_bits))
        r = lax.shift_right_logical(jnp.bitwise_and(code, 8 * blocks - 1), 3)
        return tile_score(left_ref[r], jnp.concatenate([y, y, ones], axis=0))

    def end(code, score):
        t = lax.shift_right_logical(code, slot_bits)
        own, own_total = tile_sums(score)
        at = eight_rows(jnp.where(jnp.bitwise_and(code, 7) == 7, tgt_blocks, t))
        old = high_ref[at, :]
        high = jnp.maximum(own, old)
        high_ref[at, :] = high
        total_ref[at, :] = own_total * jnp.exp2(own - high) + total_ref[at, :] * jnp.exp2(old - high)

    pipeline(list_ref, score_ref, begin, end)

    def finish(step, _):
        out_ref[eight_rows(step), :] = merged_rows(high_ref, total_ref, step, 8)
        return 0

    pieces = 4
    size = tgt_blocks // pieces
    copies = []
    for piece in range(pieces):
        lax.fori_loop(piece * size // 8, (piece + 1) * size // 8, finish, 0, unroll=8)
        rows = pl.ds(piece * size, size)
        copies.append(pltpu.make_async_copy(out_ref.at[rows], out_any.at[rows], sem.at[piece]))
        copies[-1].start()
    for copy in copies + [pot_copy]:
        copy.wait()


def remote(source, target, send_sem, recv_sem, axis, peer):
    copy = pltpu.make_async_remote_copy(
        src_ref=source,
        dst_ref=target,
        send_sem=send_sem,
        recv_sem=recv_sem,
        device_id={axis: peer},
        device_id_type=MESH,
    )
    copy.start()
    return copy


def greet(axis, peers):
    barrier = pltpu.get_barrier_semaphore()
    for peer in peers:
        pl.semaphore_signal(barrier, inc=1, device_id={axis: peer}, device_id_type=MESH)
    return lambda: pl.semaphore_wait(barrier, len(peers))


def combined(terms):
    high = functools.reduce(jnp.maximum, terms)
    return high + jnp.log2(sum(jnp.exp2(term - high) for term in terms))


def row_exchange_kernel(axis, n, part_any, out_ref, mine_ref, parts, whole, local_sem, send_sem, recv_sem, send_sem2, recv_sem2):
    me = lax.axis_index(axis)
    rows = part_any.shape[0] // n

    def chunk(i):
        return pl.ds(pl.multiple_of(i * rows, rows), rows)

    peers = [lax.rem(me + s, n) for s in range(1, n)]
    all_here = greet(axis, peers)
    mine_copy = pltpu.make_async_copy(part_any.at[chunk(me)], mine_ref, local_sem.at[0])
    mine_copy.start()
    mine_copy.wait()
    all_here()
    copies = [
        remote(part_any.at[chunk(peer)], parts.at[s], send_sem.at[s], recv_sem.at[s], axis, peer) for s, peer in enumerate(peers)
    ]
    for copy in copies:
        copy.wait_recv()
    whole[chunk(me), :] = combined([mine_ref[...]] + [parts[s] for s in range(n - 1)])
    after = [
        remote(whole.at[chunk(me)], whole.at[chunk(me)], send_sem2.at[s], recv_sem2.at[s], axis, peer) for s, peer in enumerate(peers)
    ]
    for copy in after:
        copy.wait_recv()
    out_ref[...] = whole[...]
    for copy in copies + after:
        copy.wait_send()


def row_exchange(axis, n, cid, part):
    rows = part.shape[0] // n
    return pl.pallas_call(
        functools.partial(row_exchange_kernel, axis, n),
        out_shape=jax.ShapeDtypeStruct(part.shape, F32),
        in_specs=[ANY],
        out_specs=VMEM,
        scratch_shapes=[
            pltpu.VMEM((rows, BLK), F32),
            pltpu.VMEM((n - 1, rows, BLK), F32),
            pltpu.VMEM(part.shape, F32),
            pltpu.SemaphoreType.DMA((1,)),
            pltpu.SemaphoreType.DMA((n - 1,)),
            pltpu.SemaphoreType.DMA((n - 1,)),
            pltpu.SemaphoreType.DMA((n - 1,)),
            pltpu.SemaphoreType.DMA((n - 1,)),
        ],
        compiler_params=pltpu.CompilerParams(collective_id=cid, has_side_effects=True, vmem_limit_bytes=8 * 2**20),
        name="exchange_" + axis,
    )(part)


PIECES = 4


def col_exchange_kernel(axis, n, shift, part_any, y_any, out_ref, mine_ref, twin_ref, pair_ref, parts, whole, y_ref, sq_ref, local_sem, send_a, recv_a, send_b, recv_b, send_c, recv_c, send_d, recv_d):
    me = lax.axis_index(axis)
    chips = n // 2
    core = lax.rem(me, 2)
    chip = lax.div(me, 2)
    twin = me + 1 - 2 * core
    rows = part_any.shape[0] // n
    half = chips * rows
    size = half // PIECES
    others = [lax.rem(chip + s, chips) for s in range(1, chips)]

    def chunk(where, i):
        return pl.ds(pl.multiple_of((where * chips + i) * rows, rows), rows)

    def local(i):
        return pl.ds(pl.multiple_of(i * rows, rows), rows)

    def piece(where, p):
        return pl.ds(pl.multiple_of(where * half + p * size, size), size)

    all_here = greet(axis, [twin] + [2 * other + core for other in others])
    mine_copy = pltpu.make_async_copy(part_any.at[pl.ds(pl.multiple_of(core * half, half), half)], mine_ref, local_sem.at[0])
    mine_copy.start()
    width = rows * BLK
    own = core * chips + chip
    y_copy = pltpu.make_async_copy(y_any.at[:, pl.ds(pl.multiple_of(own * width, width), width)], y_ref, local_sem.at[1])
    y_copy.start()
    y_copy.wait()
    y = y_ref[...].astype(F32)
    sq = jnp.sum(y * y, axis=0, keepdims=True) * (1.0 / (2 * y.shape[0]))
    for q in range(rows):
        sq_ref[pl.ds(q, 1), :] = sq[:, q * BLK : (q + 1) * BLK]
    mine_copy.wait()
    all_here()

    first = [
        remote(part_any.at[piece(1 - core, p)], twin_ref.at[pl.ds(p * size, size)], send_a.at[p], recv_a.at[p], axis, twin)
        for p in range(PIECES)
    ]
    for p in range(PIECES):
        first[p].wait_recv()
        at = pl.ds(p * size, size)
        pair_ref[at, :] = combined([mine_ref[at, :], twin_ref[at, :]])
    second = [
        remote(pair_ref.at[local(other)], parts.at[s], send_b.at[s], recv_b.at[s], axis, 2 * other + core)
        for s, other in enumerate(others)
    ]
    for copy in second:
        copy.wait_recv()
    result = combined([pair_ref[local(chip), :]] + [parts[s] for s in range(chips - 1)])
    mine = chunk(core, chip)
    whole[mine, :] = sq_ref[...] - FROM_LOG2 * result + shift
    third = [
        remote(whole.at[mine], whole.at[mine], send_c.at[s], recv_c.at[s], axis, 2 * other + core) for s, other in enumerate(others)
    ]
    fourth = [remote(whole.at[mine], whole.at[mine], send_d.at[chips - 1], recv_d.at[chips - 1], axis, twin)]
    for s in range(chips - 1):
        third[s].wait_recv()
        came = chunk(core, lax.rem(chip + chips - 1 - s, chips))
        fourth.append(remote(whole.at[came], whole.at[came], send_d.at[s], recv_d.at[s], axis, twin))
    for copy in fourth:
        copy.wait_recv()
    out_ref[...] = whole[...]
    for copy in first + second + third + fourth:
        copy.wait_send()


def col_exchange(axis, n, cid, shift, part, y):
    rows, chips = part.shape[0] // n, n // 2
    half = chips * rows
    sems = [pltpu.SemaphoreType.DMA((count,)) for count in (2, PIECES, PIECES, chips - 1, chips - 1, chips - 1, chips - 1, chips, chips)]
    return pl.pallas_call(
        functools.partial(col_exchange_kernel, axis, n, shift),
        out_shape=jax.ShapeDtypeStruct(part.shape, F32),
        in_specs=[ANY, ANY],
        out_specs=VMEM,
        scratch_shapes=[
            pltpu.VMEM((half, BLK), F32),
            pltpu.VMEM((half, BLK), F32),
            pltpu.VMEM((half, BLK), F32),
            pltpu.VMEM((chips - 1, rows, BLK), F32),
            pltpu.VMEM(part.shape, F32),
            pltpu.VMEM((y.shape[0], rows * BLK), BF16),
            pltpu.VMEM((rows, BLK), F32),
            *sems,
        ],
        compiler_params=pltpu.CompilerParams(collective_id=cid, has_side_effects=True, vmem_limit_bytes=8 * 2**20),
        name="exchange_" + axis,
    )(part, y)


VMEM = pl.BlockSpec(memory_space=pltpu.VMEM)
SMEM = pl.BlockSpec(memory_space=pltpu.SMEM)
ANY = pl.BlockSpec(memory_space=pl.ANY)


def row_pass(support, counts, x, y, g):
    blocks, slots = counts.shape[0], support.shape[0]
    return pl.pallas_call(
        row_kernel,
        out_shape=(jax.ShapeDtypeStruct((blocks, BLK), F32), jax.ShapeDtypeStruct((blocks * slots + 2 * GROUP + BLK,), jnp.int32)),
        in_specs=[ANY] * 5,
        out_specs=(VMEM, ANY),
        scratch_shapes=[
            pltpu.SMEM(support.shape, jnp.int32),
            pltpu.SMEM(counts.shape, jnp.int32),
            pltpu.SMEM((blocks * slots + 2 * GROUP + BLK,), jnp.int32),
            pltpu.VMEM(x.shape, BF16),
            pltpu.VMEM(y.shape, BF16),
            pltpu.VMEM(g.shape, F32),
            pltpu.VMEM((blocks, 2 * x.shape[0] + 32, BLK), BF16),
            pltpu.VMEM((blocks * 64, BLK), F32),
            pltpu.VMEM((blocks * 64, BLK), F32),
            pltpu.VMEM((GROUP, BLK, BLK), F32),
            pltpu.SemaphoreType.DMA((6,)),
        ],
        name="row_pass",
        compiler_params=pltpu.CompilerParams(vmem_limit_bytes=56 * 2**20),
    )(support, counts, x, y, g)


def col_pass(log_total, tiles, x, y, lse):
    blocks, tgt_blocks = lse.shape[0], y.shape[1] // BLK
    return pl.pallas_call(
        functools.partial(col_kernel, log_total),
        out_shape=(jax.ShapeDtypeStruct((blocks, BLK), F32), jax.ShapeDtypeStruct((tgt_blocks, BLK), F32)),
        in_specs=[ANY, VMEM, VMEM, VMEM],
        out_specs=(ANY, ANY),
        scratch_shapes=[
            pltpu.SMEM(tiles.shape, jnp.int32),
            pltpu.VMEM((blocks, BLK), F32),
            pltpu.VMEM((tgt_blocks, BLK), F32),
            pltpu.VMEM((blocks, 2 * x.shape[0] + 16, BLK), BF16),
            pltpu.VMEM((tgt_blocks * 8 + 64, BLK), F32),
            pltpu.VMEM((tgt_blocks * 8 + 64, BLK), F32),
            pltpu.VMEM((GROUP, BLK, BLK), F32),
            pltpu.SemaphoreType.DMA((6,)),
        ],
        name="col_pass",
        compiler_params=pltpu.CompilerParams(vmem_limit_bytes=40 * 2**20),
    )(tiles, x, y, lse)


def body(src_points, tgt_points, tgt_potential, support, counts):
    total_src = src_points.shape[1] * lax.axis_size("src")
    total_tgt = tgt_points.shape[1] * lax.axis_size("tgt")
    flat_support = support.transpose(2, 1, 0)
    flat_counts = counts.reshape(-1)
    row_part, tiles = row_pass(flat_support, flat_counts, src_points, tgt_points, tgt_potential.reshape(-1, BLK))
    row_lse = row_exchange("tgt", lax.axis_size("tgt"), 0, row_part)
    src_potential, col_part = col_pass(math.log(total_tgt), tiles, src_points, tgt_points, row_lse)
    new_tgt = col_exchange("src", lax.axis_size("src"), 1, BLUR * math.log(total_src), col_part, tgt_points)
    return src_potential.reshape(-1), new_tgt.reshape(-1)


def solution(mesh):
    return jax.shard_map(
        body,
        mesh=mesh,
        in_specs=(P(None, "src"), P(None, "tgt"), P("tgt"), P("src", "tgt", None), P("src", "tgt")),
        out_specs=(P("src"), P("tgt")),
        check_vma=False,
    )
```

time: 73.5 us -> 68 us (0.925)
  Pallas kernels: 69.8 us -> 64.9 us
    pallas_call x1, Pallas kernels: 15.3 us -> 11.2 us  [col_pass(): pl.pallas_call(functools.partial(col_kernel, log_total), out_shape=(jax.S...]
    pallas_call x3, Pallas kernels: 54.6 us -> 53.7 us  [the longest x1 21.9 us: col_exchange(): pl.pallas_call(functools.partial(col_exchange_kernel, axis, n, shift), ou...]
    unnamed x13 -> x9, local copies, waits for them, and re-layouts: 2.22 us -> 2.25 us
where the time goes in v3:
time: 68 us; the launch traced here: 67.8 us
  Pallas kernels  64.9 us (95%)
  local copies, waits for them, and re-layouts  2.25 us (3%)
  between operations  0.71 us (1%)
    pallas_call x1, Pallas kernels, col_exchange(): pl.pallas_call(functools.partial(col_exchange_kernel, axis, n, shift), ou...  21.9 us
    pallas_call x1, Pallas kernels, row_exchange(): pl.pallas_call(functools.partial(row_exchange_kernel, axis, n), out_shape...  16.9 us
    pallas_call x1, Pallas kernels, row_pass(): pl.pallas_call(row_kernel, out_shape=(jax.ShapeDtypeStruct((blocks, BLK),...  14.9 us
    pallas_call x1, Pallas kernels, col_pass(): pl.pallas_call(functools.partial(col_kernel, log_total), out_shape=(jax.S...  11.2 us
    unnamed x9, local copies, waits for them, and re-layouts  2.25 us

profile of v3, /device:TPU:1, one launch (start us, length us, event | category | flops | bytes accessed | tf_op | source)
XLA Modules:
  0.0 67.8 jit_solution(16257273716264216739)
XLA Ops:
  0.6 0.0 copy-start
  0.6 0.0 copy-start.1
  0.7 14.9 %row_pass.1 = (f32[128,128]{1,0:T(8,128)}, s32[960]{0:T(1024)}) custom-call(s32[6,1,128]{2,1,0:T(1,128)} %bitcast.7, s32[128]{0:T(128)} %bitcast.8, bf16[32,16384]{1,0:T(8,128)(2,1)} %x_ref.1, bf16[32,65536]{1,0:T(8,128)(2,1)} %y_any.3, f32[512,128]{1,0:T(8,128)} %bitcast.6), custom_call_target="tpu_custom_call" | custom-call | tf_op jit(solution)/shard_map/row_pass/pallas_call | solution.py:399
  15.6 0.0 copy-start.2
  15.6 0.8 %copy-done.2 = f32[128,128]{1,0:T(8,128)S(1)} copy-done((f32[128,128]{1,0:T(8,128)S(1)}, f32[128,128]{1,0:T(8,128)}, u32[]{:S(2)}) %copy-start.2) | copy-done | bytes 65560
  16.4 16.9 %exchange_tgt.1.lse_ref = f32[128,128]{1,0:T(8,128)S(1)} custom-call(f32[128,128]{1,0:T(8,128)S(1)} %copy-done.2), custom_call_target="tpu_custom_call" | custom-call | tf_op jit(solution)/shard_map/exchange_tgt/pallas_call | solution.py:278
  33.4 0.0 copy-done
  33.4 0.0 copy-done.1
  33.4 0.0 copy-start.3
  33.4 0.7 copy-done.3
  34.1 11.2 %col_pass.1 = (f32[128,128]{1,0:T(8,128)}, f32[512,128]{1,0:T(8,128)S(1)}) custom-call(s32[960]{0:T(1024)S(1)} %copy-done.3, bf16[32,16384]{1,0:T(8,128)(2,1)S(1)} %copy-done.1, bf16[32,65536]{1,0:T(8,128)(2,1)S(1)} %copy-done, f32[128,128]{1,0:T(8,128)S(1)} %exchange_tgt.1.lse_ref), custom_call_target="tpu_custom_call" | custom-call | tf_op jit(solution)/shard_map/col_pass/pallas_call | solution.py:424
  45.2 21.9 %exchange_src.1 = f32[512,128]{1,0:T(8,128)S(1)} custom-call(f32[512,128]{1,0:T(8,128)S(1)} %get-tuple-element.9.part_any, bf16[32,65536]{1,0:T(8,128)(2,1)S(1)} %copy-done), custom_call_target="tpu_custom_call" | custom-call | tf_op jit(solution)/shard_map/exchange_src/pallas_call | solution.py:372
  67.1 0.7 %copy.8 = f32[65536]{0:T(1024)} copy(f32[65536]{0:T(1024)S(1)} %bitcast.5) | data formatting | bytes 524288
Async XLA Ops:
  0.6 32.7 %copy-start = (bf16[32,65536]{1,0:T(8,128)(2,1)S(1)}, bf16[32,65536]{1,0:T(8,128)(2,1)}, u32[]{:S(2)}) copy-start(bf16[32,65536]{1,0:T(8,128)(2,1)} %y_any.3) | copy-start | bytes 12582916
  0.6 32.7 %copy-start.1 = (bf16[32,16384]{1,0:T(8,128)(2,1)S(1)}, bf16[32,16384]{1,0:T(8,128)(2,1)}, u32[]{:S(2)}) copy-start(bf16[32,16384]{1,0:T(8,128)(2,1)} %x_ref.1) | copy-start | bytes 3145732
  15.6 0.8 %copy-start.2 = (f32[128,128]{1,0:T(8,128)S(1)}, f32[128,128]{1,0:T(8,128)}, u32[]{:S(2)}) copy-start(f32[128,128]{1,0:T(8,128)} %get-tuple-element.7.part_any) | copy-start | bytes 196612
  33.4 0.7 %copy-start.3 = (s32[960]{0:T(1024)S(1)}, s32[960]{0:T(1024)}, u32[]{:S(2)}) copy-start(s32[960]{0:T(1024)} %get-tuple-element.6.list_any) | copy-start | bytes 11524

commit v4 on v3

v4 whole, which is shorter than its diff:
```python
import functools
import math

import jax
import jax.numpy as jnp
from jax import lax
from jax.experimental import pallas as pl
from jax.experimental.pallas import tpu as pltpu
from jax.sharding import PartitionSpec as P

BLK = 128
BLUR = 0.05
NEG = -1e30
TO_LOG2 = math.log2(math.e) / BLUR
FROM_LOG2 = BLUR * math.log(2.0)
GROUP = 48
BUNCH = 8
Y_PARTS = 8
F32 = jnp.float32
BF16 = jnp.bfloat16
MESH = pl.DeviceIdType.MESH


def three_parts(v):
    hi = v.astype(BF16).astype(F32)
    mid = (v - hi).astype(BF16).astype(F32)
    return hi, mid, v - hi - mid


def split_source(x, scale):
    scaled = x.astype(F32) * scale
    hi = scaled.astype(BF16)
    return hi, (scaled - hi.astype(F32)).astype(BF16)


def lane_block(ref, index):
    return ref[:, pl.ds(pl.multiple_of(index * BLK, BLK), BLK)]


def eight_rows(index):
    return pl.ds(pl.multiple_of(index * 8, 8), 8)


def tile_score(left, right):
    return lax.dot_general(left, right, (((0,), (0,)), ((), ())), preferred_element_type=F32)


def tile_sums(score):
    score = score.reshape(BLK // 8, 8, BLK)
    high = jnp.max(score, axis=0)
    return high, jnp.sum(jnp.exp2(score - high[None]), axis=0)


def pipeline(list_ref, steps, score_ref, begin, end):
    for q in range(GROUP):
        score_ref[q] = begin(list_ref[q])

    def step(i, _):
        for q in range(GROUP):
            end(list_ref[i * GROUP + q], score_ref[q])
            score_ref[q] = begin(list_ref[(i + 1) * GROUP + q])
        return 0

    lax.fori_loop(0, steps, step, 0)


def merged_rows(high_ref, total_ref, step, stride):
    at = [pl.ds(step * 8 * stride + s, 8, stride=stride) for s in range(8)]
    highs = [high_ref[a, :] for a in at]
    high = functools.reduce(jnp.maximum, highs)
    total = sum(total_ref[a, :] * jnp.exp2(h - high) for a, h in zip(at, highs))
    return jnp.where(total > 0.0, high + jnp.log2(total), NEG)


def chunk_offset(c, n):
    return lax.rem(n // 2 + lax.div(c + 1, 2) * (1 - 2 * lax.rem(c + 1, 2)) + n, n)


def row_kernel(axis, n, support_any, counts_any, x_any, y_any, g_any, out_ref, support_ref, counts_ref, x_ref, y_ref, g_ref, left_ref, right_ref, score_ref, high_ref, total_ref, part_ref, parts, whole, sem, send_sem, recv_sem, send_sem2, recv_sem2):
    blocks = out_ref.shape[0]
    slots = support_ref.shape[0]
    features = x_ref.shape[0]
    rows = blocks // n
    bunches = rows // BUNCH
    me = lax.axis_index(axis)
    tgt_blocks = g_ref.shape[0]
    wide = y_ref.shape[1] // Y_PARTS
    strips = [pl.ds(i * wide, wide) for i in range(Y_PARTS)]
    pairs = ((support_any, support_ref), (counts_any, counts_ref), (x_any, x_ref), (g_any, g_ref))
    pairs = pairs + tuple((y_any.at[:, strip], y_ref.at[:, strip]) for strip in strips)
    fetches = [pltpu.make_async_copy(a, b, sem.at[i]) for i, (a, b) in enumerate(pairs)]
    for fetch in fetches:
        fetch.start()
    all_here = greet(axis, [lax.rem(me + s, n) for s in range(1, n)])
    ones = jnp.where(lax.broadcasted_iota(jnp.int32, (32, BLK), 0) < 24, 1.0, 0.0).astype(BF16)
    fetches[2].wait()

    def prepare(r, _):
        hi, lo = split_source(lane_block(x_ref, r), TO_LOG2 / features)
        right_ref[r] = jnp.concatenate([hi, lo, ones], axis=0)
        return 0

    lax.fori_loop(0, blocks, prepare, 0, unroll=16)
    for i in (0, 1, 3):
        fetches[i].wait()

    def extend(step, _):
        pot = (TO_LOG2 / 8) * g_ref[eight_rows(step), :]
        for q in range(8):
            t = step * 8 + q
            y = lane_block(y_ref, t)
            yf = y.astype(F32)
            sq = yf * yf
            sq = functools.reduce(jnp.add, [sq[i : i + 8] for i in range(0, features, 8)])
            hi, mid, lo = three_parts(pot[q : q + 1] - (TO_LOG2 / (2 * features)) * sq)
            extra = jnp.concatenate([hi, mid, lo, jnp.zeros((8, BLK), F32)], axis=0).astype(BF16)
            left_ref[t] = jnp.concatenate([y, y, extra], axis=0)
        return 0

    each = tgt_blocks // 8 // Y_PARTS
    for i in range(Y_PARTS):
        fetches[4 + i].wait()
        lax.fori_loop(i * each, (i + 1) * each, extend, 0)
    height = left_ref.shape[1]
    first = lax.broadcasted_iota(jnp.int32, (height, BLK), 0) == 2 * features
    left_ref[tgt_blocks] = jnp.where(first, NEG, 0.0).astype(BF16)

    def chunk(i):
        return pl.ds(pl.multiple_of(i * rows, rows), rows)

    def first_row(i):
        owner = lax.rem(me + chunk_offset(lax.div(i, bunches), n), n)
        return owner * rows + lax.rem(i, bunches) * BUNCH

    def begin(r):
        lefts = [left_ref[jnp.where(k < counts_ref[r], support_ref[k, 0, r], tgt_blocks)] for k in range(slots)]
        return jnp.split(tile_score(jnp.concatenate(lefts, axis=1), right_ref[r]), slots, axis=0)

    def end(q):
        sums = [tile_sums(score_ref[q * slots + k]) for k in range(slots)]
        high = functools.reduce(jnp.maximum, [h for h, _ in sums])
        return high, sum(t * jnp.exp2(h - high) for h, t in sums)

    for q in range(BUNCH):
        for k, score in enumerate(begin(first_row(0) + q)):
            score_ref[q * slots + k] = score

    def send(c):
        target = lax.rem(me + chunk_offset(c, n), n)
        return pltpu.make_async_remote_copy(
            src_ref=part_ref.at[chunk(target)],
            dst_ref=parts.at[c],
            send_sem=send_sem.at[c],
            recv_sem=recv_sem.at[c],
            device_id={axis: target},
            device_id_type=MESH,
        )

    def chunk_step(c, _):
        def step(b, _):
            after = first_row(c * bunches + b + 1)
            for q in range(BUNCH):
                at = eight_rows(b * BUNCH + q)
                high_ref[at, :], total_ref[at, :] = end(q)
                for k, score in enumerate(begin(after + q)):
                    score_ref[q * slots + k] = score
            return 0

        lax.fori_loop(0, bunches, step, 0)
        owner = lax.rem(me + chunk_offset(c, n), n)
        for h in range(rows // 8):
            part_ref[eight_rows(owner * (rows // 8) + h), :] = merged_rows(high_ref, total_ref, h, 8)

        @pl.when(c == 0)
        def _():
            all_here()

        @pl.when(c < n - 1)
        def _():
            send(c).start()

        return 0

    lax.fori_loop(0, n, chunk_step, 0)
    for c in range(n - 1):
        send(jnp.int32(c)).wait_recv()
    whole[chunk(me), :] = combined([part_ref[chunk(me), :]] + [parts[c] for c in range(n - 1)])
    after = [
        remote(whole.at[chunk(me)], whole.at[chunk(me)], send_sem2.at[s], recv_sem2.at[s], axis, lax.rem(me + s + 1, n))
        for s in range(n - 1)
    ]
    for copy in after:
        copy.wait_recv()
    out_ref[...] = whole[...]
    for c in range(n - 1):
        send(jnp.int32(c)).wait_send()
    for copy in after:
        copy.wait_send()


def col_kernel(log_total, support_any, counts_any, x_ref, y_ref, lse_ref, pot_any, out_any, support_ref, counts_ref, list_ref, pot_ref, out_ref, left_ref, high_ref, total_ref, score_ref, sem):
    blocks = pot_ref.shape[0]
    features = x_ref.shape[0]
    tgt_blocks = out_ref.shape[0]

    slots = support_ref.shape[0]
    fetches = [
        pltpu.make_async_copy(a, b, sem.at[4 + i]) for i, (a, b) in enumerate(((support_any, support_ref), (counts_any, counts_ref)))
    ]
    for fetch in fetches:
        fetch.start()

    def clear(step, _):
        at = pl.ds(pl.multiple_of(step * 64, 64), 64)
        high_ref[at, :] = jnp.full((64, BLK), NEG, F32)
        total_ref[at, :] = jnp.zeros((64, BLK), F32)
        return 0

    lax.fori_loop(0, high_ref.shape[0] // 64, clear, 0)
    sub = lax.broadcasted_iota(jnp.int32, (16, BLK), 0)
    ones = jnp.where(sub < 3, 1.0, 0.0).astype(BF16)

    for fetch in fetches:
        fetch.wait()

    def prepare(r, tail):
        for k in range(slots):
            list_ref[tail + k] = support_ref[k, 0, r] * (8 * blocks) + (r * 8 + k)
        x = lane_block(x_ref, r)
        xf = x.astype(F32)
        pot = -FROM_LOG2 * lse_ref[pl.ds(r, 1), :] + BLUR * log_total
        pot_ref[pl.ds(r, 1), :] = pot + jnp.sum(xf * xf, axis=0, keepdims=True) * (1.0 / (2 * features))
        hi, mid, lo = three_parts(TO_LOG2 * pot)
        extra = jnp.where(sub == 0, hi, jnp.where(sub == 1, mid, jnp.where(sub == 2, lo, 0.0))).astype(BF16)
        left_ref[r] = jnp.concatenate([*split_source(x, TO_LOG2 / features), extra], axis=0)
        return tail + counts_ref[r]

    live = lax.fori_loop(0, blocks, prepare, 0, unroll=16)
    for q in range(2 * GROUP):
        list_ref[live + q] = 7
    pot_copy = pltpu.make_async_copy(pot_ref, pot_any, sem.at[6])
    pot_copy.start()

    slot_bits = (8 * blocks).bit_length() - 1

    def begin(code):
        y = lane_block(y_ref, lax.shift_right_logical(code, slot_bits))
        r = lax.shift_right_logical(jnp.bitwise_and(code, 8 * blocks - 1), 3)
        return tile_score(left_ref[r], jnp.concatenate([y, y, ones], axis=0))

    def end(code, score):
        t = lax.shift_right_logical(code, slot_bits)
        own, own_total = tile_sums(score)
        at = eight_rows(jnp.where(jnp.bitwise_and(code, 7) == 7, tgt_blocks, t))
        old = high_ref[at, :]
        high = jnp.maximum(own, old)
        high_ref[at, :] = high
        total_ref[at, :] = own_total * jnp.exp2(own - high) + total_ref[at, :] * jnp.exp2(old - high)

    pipeline(list_ref, lax.div(live + (GROUP - 1), GROUP), score_ref, begin, end)

    def finish(step, _):
        out_ref[eight_rows(step), :] = merged_rows(high_ref, total_ref, step, 8)
        return 0

    pieces = 4
    size = tgt_blocks // pieces
    copies = []
    for piece in range(pieces):
        lax.fori_loop(piece * size // 8, (piece + 1) * size // 8, finish, 0, unroll=8)
        rows = pl.ds(piece * size, size)
        copies.append(pltpu.make_async_copy(out_ref.at[rows], out_any.at[rows], sem.at[piece]))
        copies[-1].start()
    for copy in copies + [pot_copy]:
        copy.wait()


def remote(source, target, send_sem, recv_sem, axis, peer):
    copy = pltpu.make_async_remote_copy(
        src_ref=source,
        dst_ref=target,
        send_sem=send_sem,
        recv_sem=recv_sem,
        device_id={axis: peer},
        device_id_type=MESH,
    )
    copy.start()
    return copy


def greet(axis, peers):
    barrier = pltpu.get_barrier_semaphore()
    for peer in peers:
        pl.semaphore_signal(barrier, inc=1, device_id={axis: peer}, device_id_type=MESH)
    return lambda: pl.semaphore_wait(barrier, len(peers))


def combined(terms):
    high = functools.reduce(jnp.maximum, terms)
    return high + jnp.log2(sum(jnp.exp2(term - high) for term in terms))


PIECES = 4


def col_exchange_kernel(axis, n, shift, part_any, y_any, out_ref, mine_ref, twin_ref, pair_ref, parts, whole, y_ref, sq_ref, local_sem, send_a, recv_a, send_b, recv_b, send_c, recv_c, send_d, recv_d):
    me = lax.axis_index(axis)
    chips = n // 2
    core = lax.rem(me, 2)
    chip = lax.div(me, 2)
    twin = me + 1 - 2 * core
    rows = part_any.shape[0] // n
    half = chips * rows
    size = half // PIECES
    others = [lax.rem(chip + s, chips) for s in range(1, chips)]

    def chunk(where, i):
        return pl.ds(pl.multiple_of((where * chips + i) * rows, rows), rows)

    def local(i):
        return pl.ds(pl.multiple_of(i * rows, rows), rows)

    def piece(where, p):
        return pl.ds(pl.multiple_of(where * half + p * size, size), size)

    all_here = greet(axis, [twin] + [2 * other + core for other in others])
    mine_copy = pltpu.make_async_copy(part_any.at[pl.ds(pl.multiple_of(core * half, half), half)], mine_ref, local_sem.at[0])
    mine_copy.start()
    width = rows * BLK
    own = core * chips + chip
    y_copy = pltpu.make_async_copy(y_any.at[:, pl.ds(pl.multiple_of(own * width, width), width)], y_ref, local_sem.at[1])
    y_copy.start()
    y_copy.wait()
    y = y_ref[...].astype(F32)
    sq = jnp.sum(y * y, axis=0, keepdims=True) * (1.0 / (2 * y.shape[0]))
    for q in range(rows):
        sq_ref[pl.ds(q, 1), :] = sq[:, q * BLK : (q + 1) * BLK]
    mine_copy.wait()
    all_here()

    first = [
        remote(part_any.at[piece(1 - core, p)], twin_ref.at[pl.ds(p * size, size)], send_a.at[p], recv_a.at[p], axis, twin)
        for p in range(PIECES)
    ]
    for p in range(PIECES):
        first[p].wait_recv()
        at = pl.ds(p * size, size)
        pair_ref[at, :] = combined([mine_ref[at, :], twin_ref[at, :]])
    second = [
        remote(pair_ref.at[local(other)], parts.at[s], send_b.at[s], recv_b.at[s], axis, 2 * other + core)
        for s, other in enumerate(others)
    ]
    for copy in second:
        copy.wait_recv()
    result = combined([pair_ref[local(chip), :]] + [parts[s] for s in range(chips - 1)])
    mine = chunk(core, chip)
    whole[mine, :] = sq_ref[...] - FROM_LOG2 * result + shift
    third = [
        remote(whole.at[mine], whole.at[mine], send_c.at[s], recv_c.at[s], axis, 2 * other + core) for s, other in enumerate(others)
    ]
    fourth = [remote(whole.at[mine], whole.at[mine], send_d.at[chips - 1], recv_d.at[chips - 1], axis, twin)]
    for s in range(chips - 1):
        third[s].wait_recv()
        came = chunk(core, lax.rem(chip + chips - 1 - s, chips))
        fourth.append(remote(whole.at[came], whole.at[came], send_d.at[s], recv_d.at[s], axis, twin))
    for copy in fourth:
        copy.wait_recv()
    out_ref[...] = whole[...]
    for copy in first + second + third + fourth:
        copy.wait_send()


def col_exchange(axis, n, cid, shift, part, y):
    rows, chips = part.shape[0] // n, n // 2
    half = chips * rows
    sems = [pltpu.SemaphoreType.DMA((count,)) for count in (2, PIECES, PIECES, chips - 1, chips - 1, chips - 1, chips - 1, chips, chips)]
    return pl.pallas_call(
        functools.partial(col_exchange_kernel, axis, n, shift),
        out_shape=jax.ShapeDtypeStruct(part.shape, F32),
        in_specs=[ANY, ANY],
        out_specs=VMEM,
        scratch_shapes=[
            pltpu.VMEM((half, BLK), F32),
            pltpu.VMEM((half, BLK), F32),
            pltpu.VMEM((half, BLK), F32),
            pltpu.VMEM((chips - 1, rows, BLK), F32),
            pltpu.VMEM(part.shape, F32),
            pltpu.VMEM((y.shape[0], rows * BLK), BF16),
            pltpu.VMEM((rows, BLK), F32),
            *sems,
        ],
        compiler_params=pltpu.CompilerParams(collective_id=cid, has_side_effects=True, vmem_limit_bytes=8 * 2**20),
        name="exchange_" + axis,
    )(part, y)


VMEM = pl.BlockSpec(memory_space=pltpu.VMEM)
SMEM = pl.BlockSpec(memory_space=pltpu.SMEM)
ANY = pl.BlockSpec(memory_space=pl.ANY)


def row_pass(axis, n, cid, support, counts, x, y, g):
    blocks, slots = counts.shape[0], support.shape[0]
    rows = blocks // n
    return pl.pallas_call(
        functools.partial(row_kernel, axis, n),
        out_shape=jax.ShapeDtypeStruct((blocks, BLK), F32),
        in_specs=[ANY] * 5,
        out_specs=VMEM,
        scratch_shapes=[
            pltpu.SMEM(support.shape, jnp.int32),
            pltpu.SMEM(counts.shape, jnp.int32),
            pltpu.VMEM(x.shape, BF16),
            pltpu.VMEM(y.shape, BF16),
            pltpu.VMEM(g.shape, F32),
            pltpu.VMEM((g.shape[0] + 1, 2 * x.shape[0] + 32, BLK), BF16),
            pltpu.VMEM((blocks, 2 * x.shape[0] + 32, BLK), BF16),
            pltpu.VMEM((BUNCH * slots, BLK, BLK), F32),
            pltpu.VMEM((rows * 8, BLK), F32),
            pltpu.VMEM((rows * 8, BLK), F32),
            pltpu.VMEM((blocks, BLK), F32),
            pltpu.VMEM((n - 1, rows, BLK), F32),
            pltpu.VMEM((blocks, BLK), F32),
            pltpu.SemaphoreType.DMA((4 + Y_PARTS,)),
            pltpu.SemaphoreType.DMA((n - 1,)),
            pltpu.SemaphoreType.DMA((n - 1,)),
            pltpu.SemaphoreType.DMA((n - 1,)),
            pltpu.SemaphoreType.DMA((n - 1,)),
        ],
        compiler_params=pltpu.CompilerParams(collective_id=cid, has_side_effects=True, vmem_limit_bytes=40 * 2**20),
        name="row_pass",
    )(support, counts, x, y, g)


def col_pass(log_total, support, counts, x, y, lse):
    blocks, tgt_blocks = lse.shape[0], y.shape[1] // BLK
    return pl.pallas_call(
        functools.partial(col_kernel, log_total),
        out_shape=(jax.ShapeDtypeStruct((blocks, BLK), F32), jax.ShapeDtypeStruct((tgt_blocks, BLK), F32)),
        in_specs=[ANY, ANY, VMEM, VMEM, VMEM],
        out_specs=(ANY, ANY),
        scratch_shapes=[
            pltpu.SMEM(support.shape, jnp.int32),
            pltpu.SMEM(counts.shape, jnp.int32),
            pltpu.SMEM((blocks * support.shape[0] + 2 * GROUP + 8,), jnp.int32),
            pltpu.VMEM((blocks, BLK), F32),
            pltpu.VMEM((tgt_blocks, BLK), F32),
            pltpu.VMEM((blocks, 2 * x.shape[0] + 16, BLK), BF16),
            pltpu.VMEM((tgt_blocks * 8 + 64, BLK), F32),
            pltpu.VMEM((tgt_blocks * 8 + 64, BLK), F32),
            pltpu.VMEM((GROUP, BLK, BLK), F32),
            pltpu.SemaphoreType.DMA((7,)),
        ],
        name="col_pass",
        compiler_params=pltpu.CompilerParams(vmem_limit_bytes=40 * 2**20),
    )(support, counts, x, y, lse)


def body(src_points, tgt_points, tgt_potential, support, counts):
    total_src = src_points.shape[1] * lax.axis_size("src")
    total_tgt = tgt_points.shape[1] * lax.axis_size("tgt")
    flat_support = support.transpose(2, 1, 0)
    flat_counts = counts.reshape(-1)
    pot = tgt_potential.reshape(-1, BLK)
    row_lse = row_pass("tgt", lax.axis_size("tgt"), 0, flat_support, flat_counts, src_points, tgt_points, pot)
    src_potential, col_part = col_pass(math.log(total_tgt), flat_support, flat_counts, src_points, tgt_points, row_lse)
    new_tgt = col_exchange("src", lax.axis_size("src"), 1, BLUR * math.log(total_src), col_part, tgt_points)
    return src_potential.reshape(-1), new_tgt.reshape(-1)


def solution(mesh):
    return jax.shard_map(
        body,
        mesh=mesh,
        in_specs=(P(None, "src"), P(None, "tgt"), P("tgt"), P("src", "tgt", None), P("src", "tgt")),
        out_specs=(P("src"), P("tgt")),
        check_vma=False,
    )
```

time: 68 us -> 66.2 us (0.974)
  Pallas kernels: 64.9 us -> 58.9 us
  local copies, waits for them, and re-layouts: 2.25 us -> 6.41 us
    pallas_call x2 -> x1, Pallas kernels: 31.8 us -> 25.5 us  [row_pass(): pl.pallas_call(functools.partial(row_kernel, axis, n), out_shape=jax.Shap...]
    unnamed x9 -> x11, local copies, waits for them, and re-layouts: 2.25 us -> 6.41 us
    pallas_call x1, Pallas kernels: 11.2 us -> 13.1 us  [col_pass(): pl.pallas_call(functools.partial(col_kernel, log_total), out_shape=(jax.S...]
    pallas_call x1, Pallas kernels: 21.9 us -> 20.3 us  [col_exchange(): pl.pallas_call(functools.partial(col_exchange_kernel, axis, n, shift), ou...]
where the time goes in v4:
time: 66.2 us; the launch traced here: 66 us
  Pallas kernels  58.9 us (89%)
  local copies, waits for them, and re-layouts  6.41 us (10%)
  between operations  0.67 us (1%)
    pallas_call x1, Pallas kernels, row_pass(): pl.pallas_call(functools.partial(row_kernel, axis, n), out_shape=jax.Shap...  25.5 us
    pallas_call x1, Pallas kernels, col_exchange(): pl.pallas_call(functools.partial(col_exchange_kernel, axis, n, shift), ou...  20.3 us
    pallas_call x1, Pallas kernels, col_pass(): pl.pallas_call(functools.partial(col_kernel, log_total), out_shape=(jax.S...  13.1 us
    unnamed x11, local copies, waits for them, and re-layouts  6.41 us

profile of v4, /device:TPU:1, one launch (start us, length us, event | category | flops | bytes accessed | tf_op | source)
XLA Modules:
  0.0 66.0 jit_solution(458905110221581688)
XLA Ops:
  0.6 0.0 copy-start
  0.6 2.2 %copy-done = bf16[32,65536]{1,0:T(8,128)(2,1)S(1)} copy-done((bf16[32,65536]{1,0:T(8,128)(2,1)S(1)}, bf16[32,65536]{1,0:T(8,128)(2,1)}, u32[]{:S(2)}) %copy-start) | copy-done | bytes 4194328
  2.8 0.0 copy-start.1
  2.8 1.2 %copy-done.1 = bf16[32,16384]{1,0:T(8,128)(2,1)S(1)} copy-done((bf16[32,16384]{1,0:T(8,128)(2,1)S(1)}, bf16[32,16384]{1,0:T(8,128)(2,1)}, u32[]{:S(2)}) %copy-start.1) | copy-done | bytes 1048600
  4.0 0.0 copy-start.2
  4.0 0.9 %copy-done.2 = f32[65536]{0:T(1024)S(1)} copy-done((f32[65536]{0:T(1024)S(1)}, f32[65536]{0:T(1024)}, u32[]{:S(2)}) %copy-start.2) | copy-done | bytes 262168
  5.0 0.0 copy-start.3
  5.0 0.7 %copy-done.3 = s32[128,1,6]{0,1,2:T(1,128)S(1)} copy-done((s32[128,1,6]{0,1,2:T(1,128)S(1)}, s32[128,1,6]{0,1,2:T(1,128)}, u32[]{:S(2)}) %copy-start.3) | copy-done | bytes 3096
  5.7 0.0 copy-start.4
  5.7 0.7 copy-done.4
  6.3 25.5 %row_pass.1.lse_ref = f32[128,128]{1,0:T(8,128)S(1)} custom-call(s32[6,1,128]{2,1,0:T(1,128)S(1)} %bitcast.7, s32[128]{0:T(128)S(1)} %bitcast.9, bf16[32,16384]{1,0:T(8,128)(2,1)S(1)} %copy-done.1, bf16[32,65536]{1,0:T(8,128)(2,1)S(1)} %copy-done, f32[512,128]{1,0:T(8,128)S(1)} %bitcast.6), custom_call_target="tpu_custom_call" | custom-call | tf_op jit(solution)/shard_map/row_pass/pallas_call | solution.py:405
  31.9 13.1 %col_pass.1 = (f32[128,128]{1,0:T(8,128)}, f32[512,128]{1,0:T(8,128)S(1)}) custom-call(s32[6,1,128]{2,1,0:T(1,128)S(1)} %bitcast.8, s32[128]{0:T(128)S(1)} %bitcast.10, bf16[32,16384]{1,0:T(8,128)(2,1)S(1)} %copy-done.1, bf16[32,65536]{1,0:T(8,128)(2,1)S(1)} %copy-done, f32[128,128]{1,0:T(8,128)S(1)} %row_pass.1.lse_ref), custom_call_target="tpu_custom_call" | custom-call | tf_op jit(solution)/shard_map/col_pass/pallas_call | solution.py:437
  45.0 20.3 %exchange_src.1 = f32[512,128]{1,0:T(8,128)S(1)} custom-call(f32[512,128]{1,0:T(8,128)S(1)} %get-tuple-element.5.part_any, bf16[32,65536]{1,0:T(8,128)(2,1)S(1)} %copy-done), custom_call_target="tpu_custom_call" | custom-call | tf_op jit(solution)/shard_map/exchange_src/pallas_call | solution.py:377
  65.3 0.7 %copy.8 = f32[65536]{0:T(1024)} copy(f32[65536]{0:T(1024)S(1)} %bitcast.5) | data formatting | bytes 524288
Async XLA Ops:
  0.6 2.2 %copy-start = (bf16[32,65536]{1,0:T(8,128)(2,1)S(1)}, bf16[32,65536]{1,0:T(8,128)(2,1)}, u32[]{:S(2)}) copy-start(bf16[32,65536]{1,0:T(8,128)(2,1)} %y_any.3) | copy-start | bytes 12582916
  2.8 1.2 %copy-start.1 = (bf16[32,16384]{1,0:T(8,128)(2,1)S(1)}, bf16[32,16384]{1,0:T(8,128)(2,1)}, u32[]{:S(2)}) copy-start(bf16[32,16384]{1,0:T(8,128)(2,1)} %x_ref.1) | copy-start | bytes 3145732
  4.0 0.9 %copy-start.2 = (f32[65536]{0:T(1024)S(1)}, f32[65536]{0:T(1024)}, u32[]{:S(2)}) copy-start(f32[65536]{0:T(1024)} %param.7) | copy-start | bytes 786436
  5.0 0.7 %copy-start.3 = (s32[128,1,6]{0,1,2:T(1,128)S(1)}, s32[128,1,6]{0,1,2:T(1,128)}, u32[]{:S(2)}) copy-start(s32[128,1,6]{0,1,2:T(1,128)} %param.8) | copy-start | bytes 9220
  5.7 0.7 copy-start.4

commit v5 on v4

--- a/solution.py
+++ b/solution.py
@@ -13,8 +13,8 @@
 NEG = -1e30
 TO_LOG2 = math.log2(math.e) / BLUR
 FROM_LOG2 = BLUR * math.log(2.0)
-GROUP = 48
-BUNCH = 8
+GROUP = 64
+BUNCH = 16
 Y_PARTS = 8
 F32 = jnp.float32
 BF16 = jnp.bfloat16
@@ -198,17 +198,22 @@
         copy.wait_send()
 
 
-def col_kernel(log_total, support_any, counts_any, x_ref, y_ref, lse_ref, pot_any, out_any, support_ref, counts_ref, list_ref, pot_ref, out_ref, left_ref, high_ref, total_ref, score_ref, sem):
+def col_kernel(log_total, support_ref, counts_any, x_ref, y_ref, lse_ref, pot_any, out_any, turned_ref, code_ref, counts_ref, list_ref, pot_ref, out_ref, left_ref, high_ref, total_ref, score_ref, sem):
     blocks = pot_ref.shape[0]
     features = x_ref.shape[0]
     tgt_blocks = out_ref.shape[0]
 
     slots = support_ref.shape[0]
-    fetches = [
-        pltpu.make_async_copy(a, b, sem.at[4 + i]) for i, (a, b) in enumerate(((support_any, support_ref), (counts_any, counts_ref)))
+    counts_copy = pltpu.make_async_copy(counts_any, counts_ref, sem.at[4])
+    counts_copy.start()
+    row = lax.broadcasted_iota(jnp.int32, support_ref.shape, 2)
+    slot = lax.broadcasted_iota(jnp.int32, support_ref.shape, 0)
+    turned_ref[...] = support_ref[...] * (8 * blocks) + (row * 8 + slot)
+    code_copies = [
+        pltpu.make_async_copy(turned_ref.at[k, 0], code_ref.at[pl.ds(k * blocks, blocks)], sem.at[7 + k]) for k in range(slots)
     ]
-    for fetch in fetches:
-        fetch.start()
+    for copy in code_copies:
+        copy.start()
 
     def clear(step, _):
         at = pl.ds(pl.multiple_of(step * 64, 64), 64)
@@ -220,12 +225,12 @@
     sub = lax.broadcasted_iota(jnp.int32, (16, BLK), 0)
     ones = jnp.where(sub < 3, 1.0, 0.0).astype(BF16)
 
-    for fetch in fetches:
-        fetch.wait()
+    for copy in [counts_copy] + code_copies:
+        copy.wait()
 
     def prepare(r, tail):
         for k in range(slots):
-            list_ref[tail + k] = support_ref[k, 0, r] * (8 * blocks) + (r * 8 + k)
+            list_ref[tail + k] = code_ref[k * blocks + r]
         x = lane_block(x_ref, r)
         xf = x.astype(F32)
         pot = -FROM_LOG2 * lse_ref[pl.ds(r, 1), :] + BLUR * log_total
@@ -427,7 +432,7 @@
             pltpu.SemaphoreType.DMA((n - 1,)),
             pltpu.SemaphoreType.DMA((n - 1,)),
         ],
-        compiler_params=pltpu.CompilerParams(collective_id=cid, has_side_effects=True, vmem_limit_bytes=40 * 2**20),
+        compiler_params=pltpu.CompilerParams(collective_id=cid, has_side_effects=True, vmem_limit_bytes=56 * 2**20),
         name="row_pass",
     )(support, counts, x, y, g)
 
@@ -437,10 +442,11 @@
     return pl.pallas_call(
         functools.partial(col_kernel, log_total),
         out_shape=(jax.ShapeDtypeStruct((blocks, BLK), F32), jax.ShapeDtypeStruct((tgt_blocks, BLK), F32)),
-        in_specs=[ANY, ANY, VMEM, VMEM, VMEM],
+        in_specs=[VMEM, ANY, VMEM, VMEM, VMEM],
         out_specs=(ANY, ANY),
         scratch_shapes=[
-            pltpu.SMEM(support.shape, jnp.int32),
+            pltpu.VMEM(support.shape, jnp.int32),
+            pltpu.SMEM((blocks * support.shape[0],), jnp.int32),
             pltpu.SMEM(counts.shape, jnp.int32),
             pltpu.SMEM((blocks * support.shape[0] + 2 * GROUP + 8,), jnp.int32),
             pltpu.VMEM((blocks, BLK), F32),
@@ -449,7 +455,7 @@
             pltpu.VMEM((tgt_blocks * 8 + 64, BLK), F32),
             pltpu.VMEM((tgt_blocks * 8 + 64, BLK), F32),
             pltpu.VMEM((GROUP, BLK, BLK), F32),
-            pltpu.SemaphoreType.DMA((7,)),
+            pltpu.SemaphoreType.DMA((7 + support.shape[0],)),
         ],
         name="col_pass",
         compiler_params=pltpu.CompilerParams(vmem_limit_bytes=40 * 2**20),

time: 66.2 us -> 61.2 us (0.924)
  local copies, waits for them, and re-layouts: 6.41 us -> 1.57 us
    unnamed x11, local copies, waits for them, and re-layouts: 6.41 us -> 1.57 us
    pallas_call x1, Pallas kernels: 13.1 us -> 12 us  [col_pass(): pl.pallas_call(functools.partial(col_kernel, log_total), out_shape=(jax.S...]
    pallas_call x1, Pallas kernels: 25.5 us -> 26.3 us  [row_pass(): pl.pallas_call(functools.partial(row_kernel, axis, n), out_shape=jax.Shap...]
where the time goes in v5:
time: 61.2 us; the launch traced here: 61.1 us
  Pallas kernels  58.8 us (96%)
  local copies, waits for them, and re-layouts  1.57 us (3%)
  between operations  0.73 us (1%)
    pallas_call x1, Pallas kernels, row_pass(): pl.pallas_call(functools.partial(row_kernel, axis, n), out_shape=jax.Shap...  26.3 us
    pallas_call x1, Pallas kernels, col_exchange(): pl.pallas_call(functools.partial(col_exchange_kernel, axis, n, shift), ou...  20.5 us
    pallas_call x1, Pallas kernels, col_pass(): pl.pallas_call(functools.partial(col_kernel, log_total), out_shape=(jax.S...  12 us
    unnamed x11, local copies, waits for them, and re-layouts  1.57 us

profile of v5, /device:TPU:1, one launch (start us, length us, event | category | flops | bytes accessed | tf_op | source)
XLA Modules:
  0.0 61.1 jit_solution(8250654280841113989)
XLA Ops:
  0.6 0.0 copy-start
  0.6 0.0 copy-start.1
  0.7 0.0 copy-start.4
  0.7 0.0 copy-start.3
  0.7 26.3 %row_pass.1.lse_ref = f32[128,128]{1,0:T(8,128)} custom-call(s32[6,1,128]{2,1,0:T(1,128)} %bitcast.6, s32[128]{0:T(128)} %bitcast.8, bf16[32,16384]{1,0:T(8,128)(2,1)} %x_ref.1, bf16[32,65536]{1,0:T(8,128)(2,1)} %y_any.3, f32[512,128]{1,0:T(8,128)} %bitcast.10), custom_call_target="tpu_custom_call" | custom-call | tf_op jit(solution)/shard_map/row_pass/pallas_call | solution.py:410
  27.0 0.0 copy-done
  27.0 0.0 copy-done.1
  27.0 0.0 copy-done.4
  27.1 0.0 copy-done.3
  27.1 0.0 copy-start.2
  27.1 0.8 %copy-done.2 = f32[128,128]{1,0:T(8,128)S(1)} copy-done((f32[128,128]{1,0:T(8,128)S(1)}, f32[128,128]{1,0:T(8,128)}, u32[]{:S(2)}) %copy-start.2) | copy-done | bytes 65560
  27.9 12.0 %col_pass.1 = (f32[128,128]{1,0:T(8,128)}, f32[512,128]{1,0:T(8,128)S(1)}) custom-call(s32[6,1,128]{2,1,0:T(1,128)S(1)} %bitcast.7, s32[128]{0:T(128)S(1)} %bitcast.9, bf16[32,16384]{1,0:T(8,128)(2,1)S(1)} %copy-done.1, bf16[32,65536]{1,0:T(8,128)(2,1)S(1)} %copy-done, f32[128,128]{1,0:T(8,128)S(1)} %copy-done.2), custom_call_target="tpu_custom_call" | custom-call | tf_op jit(solution)/shard_map/col_pass/pallas_call | solution.py:442
  39.9 20.5 %exchange_src.1 = f32[512,128]{1,0:T(8,128)S(1)} custom-call(f32[512,128]{1,0:T(8,128)S(1)} %get-tuple-element.5.part_any, bf16[32,65536]{1,0:T(8,128)(2,1)S(1)} %copy-done), custom_call_target="tpu_custom_call" | custom-call | tf_op jit(solution)/shard_map/exchange_src/pallas_call | solution.py:382
  60.4 0.7 %copy.8 = f32[65536]{0:T(1024)} copy(f32[65536]{0:T(1024)S(1)} %bitcast.5) | data formatting | bytes 524288
Async XLA Ops:
  0.6 26.4 %copy-start = (bf16[32,65536]{1,0:T(8,128)(2,1)S(1)}, bf16[32,65536]{1,0:T(8,128)(2,1)}, u32[]{:S(2)}) copy-start(bf16[32,65536]{1,0:T(8,128)(2,1)} %y_any.3) | copy-start | bytes 12582916
  0.6 26.4 %copy-start.1 = (bf16[32,16384]{1,0:T(8,128)(2,1)S(1)}, bf16[32,16384]{1,0:T(8,128)(2,1)}, u32[]{:S(2)}) copy-start(bf16[32,16384]{1,0:T(8,128)(2,1)} %x_ref.1) | copy-start | bytes 3145732
  0.7 26.4 %copy-start.4 = (s32[128,1]{0,1:T(1,128)S(1)}, s32[128,1]{0,1:T(1,128)}, u32[]{:S(2)}) copy-start(s32[128,1]{0,1:T(1,128)} %param.9) | copy-start | bytes 1540
  0.7 26.4 %copy-start.3 = (s32[128,1,6]{0,1,2:T(1,128)S(1)}, s32[128,1,6]{0,1,2:T(1,128)}, u32[]{:S(2)}) copy-start(s32[128,1,6]{0,1,2:T(1,128)} %param.8) | copy-start | bytes 9220
  27.1 0.8 %copy-start.2 = (f32[128,128]{1,0:T(8,128)S(1)}, f32[128,128]{1,0:T(8,128)}, u32[]{:S(2)}) copy-start(f32[128,128]{1,0:T(8,128)} %row_pass.1.lse_ref) | copy-start | bytes 196612

commit v6 on v5

--- a/solution.py
+++ b/solution.py
@@ -186,7 +186,7 @@
         send(jnp.int32(c)).wait_recv()
     whole[chunk(me), :] = combined([part_ref[chunk(me), :]] + [parts[c] for c in range(n - 1)])
     after = [
-        remote(whole.at[chunk(me)], whole.at[chunk(me)], send_sem2.at[s], recv_sem2.at[s], axis, lax.rem(me + s + 1, n))
+        remote(whole.at[chunk(me)], whole.at[chunk(me)], send_sem2.at[s], recv_sem2.at[s], axis, lax.rem(me + chunk_offset(s, n), n))
         for s in range(n - 1)
     ]
     for copy in after:
@@ -308,7 +308,16 @@
 PIECES = 4
 
 
-def col_exchange_kernel(axis, n, shift, part_any, y_any, out_ref, mine_ref, twin_ref, pair_ref, parts, whole, y_ref, sq_ref, local_sem, send_a, recv_a, send_b, recv_b, send_c, recv_c, send_d, recv_d):
+def hops(step, side):
+    return sum(min(d, side - d) for d in step)
+
+
+def far_count(steps, side):
+    return sum(hops(step, side) >= 3 for step in steps)
+
+
+def col_exchange_kernel(axis, n, shift, part_any, y_any, out_ref, mine_ref, twin_ref, pair_ref, parts, far_parts, whole, y_ref, sq_ref, local_sem, *sems):
+    send_a, recv_a, send_b, recv_b, send_c, recv_c, send_d, recv_d, send_e, recv_e, send_f, recv_f = sems
     me = lax.axis_index(axis)
     chips = n // 2
     core = lax.rem(me, 2)
@@ -317,7 +326,16 @@
     rows = part_any.shape[0] // n
     half = chips * rows
     size = half // PIECES
-    others = [lax.rem(chip + s, chips) for s in range(1, chips)]
+    side = math.isqrt(chips)
+    steps = [(dy, dx) for dy in range(side) for dx in range(side)]
+    steps = sorted(steps, key=lambda step: -hops(step, side))[:-1]
+    far = far_count(steps, side)
+
+    def chip_at(dy, dx):
+        return lax.rem(lax.div(chip, side) + side + dy, side) * side + lax.rem(chip + side + dx, side)
+
+    others = [chip_at(dy, dx) for dy, dx in steps]
+    senders = [chip_at(-dy, -dx) for dy, dx in steps]
 
     def chunk(where, i):
         return pl.ds(pl.multiple_of((where * chips + i) * rows, rows), rows)
@@ -328,7 +346,9 @@
     def piece(where, p):
         return pl.ds(pl.multiple_of(where * half + p * size, size), size)
 
-    all_here = greet(axis, [twin] + [2 * other + core for other in others])
+    same = [2 * other + core for other in others]
+    across = [2 * other + 1 - core for other in others[:far]]
+    all_here = greet(axis, same + across + [twin])
     mine_copy = pltpu.make_async_copy(part_any.at[pl.ds(pl.multiple_of(core * half, half), half)], mine_ref, local_sem.at[0])
     mine_copy.start()
     width = rows * BLK
@@ -347,38 +367,48 @@
         remote(part_any.at[piece(1 - core, p)], twin_ref.at[pl.ds(p * size, size)], send_a.at[p], recv_a.at[p], axis, twin)
         for p in range(PIECES)
     ]
+    for s in range(far):
+        for j, (where, peer) in enumerate(((core, same[s]), (1 - core, across[s]))):
+            source = part_any.at[chunk(where, others[s])]
+            first.append(remote(source, far_parts.at[2 * s + j], send_e.at[2 * s + j], recv_e.at[2 * s + j], axis, peer))
     for p in range(PIECES):
         first[p].wait_recv()
         at = pl.ds(p * size, size)
         pair_ref[at, :] = combined([mine_ref[at, :], twin_ref[at, :]])
     second = [
-        remote(pair_ref.at[local(other)], parts.at[s], send_b.at[s], recv_b.at[s], axis, 2 * other + core)
-        for s, other in enumerate(others)
+        remote(pair_ref.at[local(others[s])], parts.at[s - far], send_b.at[s], recv_b.at[s], axis, same[s])
+        for s in range(far, chips - 1)
     ]
-    for copy in second:
+    for copy in first[PIECES:] + second:
         copy.wait_recv()
-    result = combined([pair_ref[local(chip), :]] + [parts[s] for s in range(chips - 1)])
+    terms = [parts[s] for s in range(chips - 1 - far)] + [far_parts[s] for s in range(2 * far)]
+    result = combined([pair_ref[local(chip), :]] + terms)
     mine = chunk(core, chip)
     whole[mine, :] = sq_ref[...] - FROM_LOG2 * result + shift
-    third = [
-        remote(whole.at[mine], whole.at[mine], send_c.at[s], recv_c.at[s], axis, 2 * other + core) for s, other in enumerate(others)
-    ]
+    third, crossing = [], []
+    for s in range(chips - 1):
+        third.append(remote(whole.at[mine], whole.at[mine], send_c.at[s], recv_c.at[s], axis, same[s]))
+        if s < far:
+            crossing.append(remote(whole.at[mine], whole.at[mine], send_f.at[s], recv_f.at[s], axis, across[s]))
     fourth = [remote(whole.at[mine], whole.at[mine], send_d.at[chips - 1], recv_d.at[chips - 1], axis, twin)]
-    for s in range(chips - 1):
+    for s in reversed(range(far, chips - 1)):
         third[s].wait_recv()
-        came = chunk(core, lax.rem(chip + chips - 1 - s, chips))
+        came = chunk(core, senders[s])
         fourth.append(remote(whole.at[came], whole.at[came], send_d.at[s], recv_d.at[s], axis, twin))
-    for copy in fourth:
+    for copy in third[:far] + crossing + fourth:
         copy.wait_recv()
     out_ref[...] = whole[...]
-    for copy in first + second + third + fourth:
+    for copy in first + second + third + crossing + fourth:
         copy.wait_send()
 
 
 def col_exchange(axis, n, cid, shift, part, y):
     rows, chips = part.shape[0] // n, n // 2
     half = chips * rows
-    sems = [pltpu.SemaphoreType.DMA((count,)) for count in (2, PIECES, PIECES, chips - 1, chips - 1, chips - 1, chips - 1, chips, chips)]
+    side = math.isqrt(chips)
+    far = far_count([(dy, dx) for dy in range(side) for dx in range(side)], side)
+    counts = (PIECES, chips - 1, chips - 1, chips, 2 * far, far)
+    sems = [pltpu.SemaphoreType.DMA((2,))] + [pltpu.SemaphoreType.DMA((count,)) for count in counts for _ in range(2)]
     return pl.pallas_call(
         functools.partial(col_exchange_kernel, axis, n, shift),
         out_shape=jax.ShapeDtypeStruct(part.shape, F32),
@@ -388,7 +418,8 @@
             pltpu.VMEM((half, BLK), F32),
             pltpu.VMEM((half, BLK), F32),
             pltpu.VMEM((half, BLK), F32),
-            pltpu.VMEM((chips - 1, rows, BLK), F32),
+            pltpu.VMEM((chips - 1 - far, rows, BLK), F32),
+            pltpu.VMEM((2 * far, rows, BLK), F32),
             pltpu.VMEM(part.shape, F32),
             pltpu.VMEM((y.shape[0], rows * BLK), BF16),
             pltpu.VMEM((rows, BLK), F32),

time: 61.2 us -> 62.1 us (1.015)
  Pallas kernels: 58.8 us -> 59.7 us
    pallas_call x1, Pallas kernels: 20.5 us -> 21.7 us  [col_exchange(): pl.pallas_call(functools.partial(col_exchange_kernel, axis, n, shift), ou...]
where the time goes in v6:
time: 62.1 us; the launch traced here: 62 us
  Pallas kernels  59.7 us (96%)
  local copies, waits for them, and re-layouts  1.57 us (3%)
  between operations  0.73 us (1%)
    pallas_call x1, Pallas kernels, row_pass(): pl.pallas_call(functools.partial(row_kernel, axis, n), out_shape=jax.Shap...  26 us
    pallas_call x1, Pallas kernels, col_exchange(): pl.pallas_call(functools.partial(col_exchange_kernel, axis, n, shift), ou...  21.7 us
    pallas_call x1, Pallas kernels, col_pass(): pl.pallas_call(functools.partial(col_kernel, log_total), out_shape=(jax.S...  12 us
    unnamed x11, local copies, waits for them, and re-layouts  1.57 us

profile of v6, /device:TPU:1, one launch (start us, length us, event | category | flops | bytes accessed | tf_op | source)
XLA Modules:
  0.0 62.0 jit_solution(4249280136542447312)
XLA Ops:
  0.6 0.0 copy-start
  0.6 0.0 copy-start.1
  0.7 0.0 copy-start.4
  0.7 0.0 copy-start.3
  0.7 26.0 %row_pass.1.lse_ref = f32[128,128]{1,0:T(8,128)} custom-call(s32[6,1,128]{2,1,0:T(1,128)} %bitcast.6, s32[128]{0:T(128)} %bitcast.8, bf16[32,16384]{1,0:T(8,128)(2,1)} %x_ref.1, bf16[32,65536]{1,0:T(8,128)(2,1)} %y_any.3, f32[512,128]{1,0:T(8,128)} %bitcast.10), custom_call_target="tpu_custom_call" | custom-call | tf_op jit(solution)/shard_map/row_pass/pallas_call | solution.py:441
  26.7 0.0 copy-done
  26.7 0.0 copy-done.1
  26.7 0.0 copy-done.4
  26.7 0.0 copy-done.3
  26.7 0.0 copy-start.2
  26.7 0.8 %copy-done.2 = f32[128,128]{1,0:T(8,128)S(1)} copy-done((f32[128,128]{1,0:T(8,128)S(1)}, f32[128,128]{1,0:T(8,128)}, u32[]{:S(2)}) %copy-start.2) | copy-done | bytes 65560
  27.6 12.0 %col_pass.1 = (f32[128,128]{1,0:T(8,128)}, f32[512,128]{1,0:T(8,128)S(1)}) custom-call(s32[6,1,128]{2,1,0:T(1,128)S(1)} %bitcast.7, s32[128]{0:T(128)S(1)} %bitcast.9, bf16[32,16384]{1,0:T(8,128)(2,1)S(1)} %copy-done.1, bf16[32,65536]{1,0:T(8,128)(2,1)S(1)} %copy-done, f32[128,128]{1,0:T(8,128)S(1)} %copy-done.2), custom_call_target="tpu_custom_call" | custom-call | tf_op jit(solution)/shard_map/col_pass/pallas_call | solution.py:473
  39.5 21.7 %exchange_src.1 = f32[512,128]{1,0:T(8,128)S(1)} custom-call(f32[512,128]{1,0:T(8,128)S(1)} %get-tuple-element.5.part_any, bf16[32,65536]{1,0:T(8,128)(2,1)S(1)} %copy-done), custom_call_target="tpu_custom_call" | custom-call | tf_op jit(solution)/shard_map/exchange_src/pallas_call | solution.py:412
  61.3 0.7 %copy.8 = f32[65536]{0:T(1024)} copy(f32[65536]{0:T(1024)S(1)} %bitcast.5) | data formatting | bytes 524288
Async XLA Ops:
  0.6 26.1 %copy-start = (bf16[32,65536]{1,0:T(8,128)(2,1)S(1)}, bf16[32,65536]{1,0:T(8,128)(2,1)}, u32[]{:S(2)}) copy-start(bf16[32,65536]{1,0:T(8,128)(2,1)} %y_any.3) | copy-start | bytes 12582916
  0.6 26.1 %copy-start.1 = (bf16[32,16384]{1,0:T(8,128)(2,1)S(1)}, bf16[32,16384]{1,0:T(8,128)(2,1)}, u32[]{:S(2)}) copy-start(bf16[32,16384]{1,0:T(8,128)(2,1)} %x_ref.1) | copy-start | bytes 3145732
  0.7 26.1 %copy-start.4 = (s32[128,1]{0,1:T(1,128)S(1)}, s32[128,1]{0,1:T(1,128)}, u32[]{:S(2)}) copy-start(s32[128,1]{0,1:T(1,128)} %param.9) | copy-start | bytes 1540
  0.7 26.1 %copy-start.3 = (s32[128,1,6]{0,1,2:T(1,128)S(1)}, s32[128,1,6]{0,1,2:T(1,128)}, u32[]{:S(2)}) copy-start(s32[128,1,6]{0,1,2:T(1,128)} %param.8) | copy-start | bytes 9220
  26.7 0.8 %copy-start.2 = (f32[128,128]{1,0:T(8,128)S(1)}, f32[128,128]{1,0:T(8,128)}, u32[]{:S(2)}) copy-start(f32[128,128]{1,0:T(8,128)} %row_pass.1.lse_ref) | copy-start | bytes 196612

commit v7 on v5

--- a/solution.py
+++ b/solution.py
@@ -61,7 +61,8 @@
             score_ref[q] = begin(list_ref[(i + 1) * GROUP + q])
         return 0
 
-    lax.fori_loop(0, steps, step, 0)
+    step(0, 0)
+    lax.fori_loop(1, steps, step, 0)
 
 
 def merged_rows(high_ref, total_ref, step, stride):
@@ -156,37 +157,38 @@
             device_id_type=MESH,
         )
 
-    def chunk_step(c, _):
-        def step(b, _):
+    def sums(c):
+        def step(b):
             after = first_row(c * bunches + b + 1)
             for q in range(BUNCH):
                 at = eight_rows(b * BUNCH + q)
                 high_ref[at, :], total_ref[at, :] = end(q)
                 for k, score in enumerate(begin(after + q)):
                     score_ref[q * slots + k] = score
-            return 0
-
-        lax.fori_loop(0, bunches, step, 0)
+
+        for b in range(bunches):
+            step(b)
+
+    def settle(c):
         owner = lax.rem(me + chunk_offset(c, n), n)
         for h in range(rows // 8):
             part_ref[eight_rows(owner * (rows // 8) + h), :] = merged_rows(high_ref, total_ref, h, 8)
 
-        @pl.when(c == 0)
-        def _():
-            all_here()
-
-        @pl.when(c < n - 1)
-        def _():
-            send(c).start()
-
-        return 0
-
-    lax.fori_loop(0, n, chunk_step, 0)
+    def chunk_step(c, _):
+        settle(c - 1)
+        send(c - 1).start()
+        sums(c)
+        return 0
+
+    sums(0)
+    all_here()
+    lax.fori_loop(1, n, chunk_step, 0)
+    settle(n - 1)
     for c in range(n - 1):
         send(jnp.int32(c)).wait_recv()
     whole[chunk(me), :] = combined([part_ref[chunk(me), :]] + [parts[c] for c in range(n - 1)])
     after = [
-        remote(whole.at[chunk(me)], whole.at[chunk(me)], send_sem2.at[s], recv_sem2.at[s], axis, lax.rem(me + s + 1, n))
+        remote(whole.at[chunk(me)], whole.at[chunk(me)], send_sem2.at[s], recv_sem2.at[s], axis, lax.rem(me + chunk_offset(s, n), n))
         for s in range(n - 1)
     ]
     for copy in after:
@@ -317,7 +319,15 @@
     rows = part_any.shape[0] // n
     half = chips * rows
     size = half // PIECES
-    others = [lax.rem(chip + s, chips) for s in range(1, chips)]
+    side = math.isqrt(chips)
+    steps = [(dy, dx) for dy in range(side) for dx in range(side)]
+    steps = sorted(steps, key=lambda step: -sum(min(d, side - d) for d in step))[:-1]
+
+    def chip_at(dy, dx):
+        return lax.rem(lax.div(chip, side) + side + dy, side) * side + lax.rem(chip + side + dx, side)
+
+    others = [chip_at(dy, dx) for dy, dx in steps]
+    senders = [chip_at(-dy, -dx) for dy, dx in steps]
 
     def chunk(where, i):
         return pl.ds(pl.multiple_of((where * chips + i) * rows, rows), rows)
@@ -364,9 +374,9 @@
         remote(whole.at[mine], whole.at[mine], send_c.at[s], recv_c.at[s], axis, 2 * other + core) for s, other in enumerate(others)
     ]
     fourth = [remote(whole.at[mine], whole.at[mine], send_d.at[chips - 1], recv_d.at[chips - 1], axis, twin)]
-    for s in range(chips - 1):
+    for s in reversed(range(chips - 1)):
         third[s].wait_recv()
-        came = chunk(core, lax.rem(chip + chips - 1 - s, chips))
+        came = chunk(core, senders[s])
         fourth.append(remote(whole.at[came], whole.at[came], send_d.at[s], recv_d.at[s], axis, twin))
     for copy in fourth:
         copy.wait_recv()

time: 61.2 us -> 60.2 us (0.984)
  Pallas kernels: 58.8 us -> 57.7 us
where the time goes in v7:
time: 60.2 us; the launch traced here: 60 us
  Pallas kernels  57.7 us (96%)
  local copies, waits for them, and re-layouts  1.57 us (3%)
  between operations  0.73 us (1%)
    pallas_call x1, Pallas kernels, row_pass(): pl.pallas_call(functools.partial(row_kernel, axis, n), out_shape=jax.Shap...  26.1 us
    pallas_call x1, Pallas kernels, col_exchange(): pl.pallas_call(functools.partial(col_exchange_kernel, axis, n, shift), ou...  20 us
    pallas_call x1, Pallas kernels, col_pass(): pl.pallas_call(functools.partial(col_kernel, log_total), out_shape=(jax.S...  11.7 us
    unnamed x11, local copies, waits for them, and re-layouts  1.57 us

profile of v7, /device:TPU:1, one launch (start us, length us, event | category | flops | bytes accessed | tf_op | source)
XLA Modules:
  0.0 60.0 jit_solution(2471884394510610813)
XLA Ops:
  0.6 0.0 copy-start
  0.6 0.0 copy-start.1
  0.7 0.0 copy-start.4
  0.7 0.0 copy-start.3
  0.7 26.1 %row_pass.1.lse_ref = f32[128,128]{1,0:T(8,128)} custom-call(s32[6,1,128]{2,1,0:T(1,128)} %bitcast.6, s32[128]{0:T(128)} %bitcast.8, bf16[32,16384]{1,0:T(8,128)(2,1)} %x_ref.1, bf16[32,65536]{1,0:T(8,128)(2,1)} %y_any.3, f32[512,128]{1,0:T(8,128)} %bitcast.10), custom_call_target="tpu_custom_call" | custom-call | tf_op jit(solution)/shard_map/row_pass/pallas_call | solution.py:420
  26.7 0.0 copy-done
  26.7 0.0 copy-done.1
  26.8 0.0 copy-done.4
  26.8 0.0 copy-done.3
  26.8 0.0 copy-start.2
  26.8 0.8 %copy-done.2 = f32[128,128]{1,0:T(8,128)S(1)} copy-done((f32[128,128]{1,0:T(8,128)S(1)}, f32[128,128]{1,0:T(8,128)}, u32[]{:S(2)}) %copy-start.2) | copy-done | bytes 65560
  27.6 11.7 %col_pass.1 = (f32[128,128]{1,0:T(8,128)}, f32[512,128]{1,0:T(8,128)S(1)}) custom-call(s32[6,1,128]{2,1,0:T(1,128)S(1)} %bitcast.7, s32[128]{0:T(128)S(1)} %bitcast.9, bf16[32,16384]{1,0:T(8,128)(2,1)S(1)} %copy-done.1, bf16[32,65536]{1,0:T(8,128)(2,1)S(1)} %copy-done, f32[128,128]{1,0:T(8,128)S(1)} %copy-done.2), custom_call_target="tpu_custom_call" | custom-call | tf_op jit(solution)/shard_map/col_pass/pallas_call | solution.py:452
  39.3 20.0 %exchange_src.1 = f32[512,128]{1,0:T(8,128)S(1)} custom-call(f32[512,128]{1,0:T(8,128)S(1)} %get-tuple-element.5.part_any, bf16[32,65536]{1,0:T(8,128)(2,1)S(1)} %copy-done), custom_call_target="tpu_custom_call" | custom-call | tf_op jit(solution)/shard_map/exchange_src/pallas_call | solution.py:392
  59.3 0.7 %copy.8 = f32[65536]{0:T(1024)} copy(f32[65536]{0:T(1024)S(1)} %bitcast.5) | data formatting | bytes 524288
Async XLA Ops:
  0.6 26.1 %copy-start = (bf16[32,65536]{1,0:T(8,128)(2,1)S(1)}, bf16[32,65536]{1,0:T(8,128)(2,1)}, u32[]{:S(2)}) copy-start(bf16[32,65536]{1,0:T(8,128)(2,1)} %y_any.3) | copy-start | bytes 12582916
  0.6 26.1 %copy-start.1 = (bf16[32,16384]{1,0:T(8,128)(2,1)S(1)}, bf16[32,16384]{1,0:T(8,128)(2,1)}, u32[]{:S(2)}) copy-start(bf16[32,16384]{1,0:T(8,128)(2,1)} %x_ref.1) | copy-start | bytes 3145732
  0.7 26.1 %copy-start.4 = (s32[128,1]{0,1:T(1,128)S(1)}, s32[128,1]{0,1:T(1,128)}, u32[]{:S(2)}) copy-start(s32[128,1]{0,1:T(1,128)} %param.9) | copy-start | bytes 1540
  0.7 26.1 %copy-start.3 = (s32[128,1,6]{0,1,2:T(1,128)S(1)}, s32[128,1,6]{0,1,2:T(1,128)}, u32[]{:S(2)}) copy-start(s32[128,1,6]{0,1,2:T(1,128)} %param.8) | copy-start | bytes 9220
  26.8 0.8 %copy-start.2 = (f32[128,128]{1,0:T(8,128)S(1)}, f32[128,128]{1,0:T(8,128)}, u32[]{:S(2)}) copy-start(f32[128,128]{1,0:T(8,128)} %row_pass.1.lse_ref) | copy-start | bytes 196612

commit v8 on v7

--- a/solution.py
+++ b/solution.py
@@ -77,7 +77,7 @@
     return lax.rem(n // 2 + lax.div(c + 1, 2) * (1 - 2 * lax.rem(c + 1, 2)) + n, n)
 
 
-def row_kernel(axis, n, support_any, counts_any, x_any, y_any, g_any, out_ref, support_ref, counts_ref, x_ref, y_ref, g_ref, left_ref, right_ref, score_ref, high_ref, total_ref, part_ref, parts, whole, sem, send_sem, recv_sem, send_sem2, recv_sem2):
+def row_kernel(axis, n, support_any, counts_any, x_any, y_any, g_any, out_ref, support_ref, counts_ref, x_ref, y_ref, g_ref, left_ref, score_ref, high_ref, total_ref, part_ref, parts, whole, sem, send_sem, recv_sem, send_sem2, recv_sem2):
     blocks = out_ref.shape[0]
     slots = support_ref.shape[0]
     features = x_ref.shape[0]
@@ -87,22 +87,14 @@
     tgt_blocks = g_ref.shape[0]
     wide = y_ref.shape[1] // Y_PARTS
     strips = [pl.ds(i * wide, wide) for i in range(Y_PARTS)]
-    pairs = ((support_any, support_ref), (counts_any, counts_ref), (x_any, x_ref), (g_any, g_ref))
-    pairs = pairs + tuple((y_any.at[:, strip], y_ref.at[:, strip]) for strip in strips)
+    pairs = ((support_any, support_ref), (counts_any, counts_ref), (g_any, g_ref))
+    pairs = pairs + tuple((y_any.at[:, strip], y_ref.at[:, strip]) for strip in strips) + ((x_any, x_ref),)
     fetches = [pltpu.make_async_copy(a, b, sem.at[i]) for i, (a, b) in enumerate(pairs)]
     for fetch in fetches:
         fetch.start()
     all_here = greet(axis, [lax.rem(me + s, n) for s in range(1, n)])
     ones = jnp.where(lax.broadcasted_iota(jnp.int32, (32, BLK), 0) < 24, 1.0, 0.0).astype(BF16)
-    fetches[2].wait()
-
-    def prepare(r, _):
-        hi, lo = split_source(lane_block(x_ref, r), TO_LOG2 / features)
-        right_ref[r] = jnp.concatenate([hi, lo, ones], axis=0)
-        return 0
-
-    lax.fori_loop(0, blocks, prepare, 0, unroll=16)
-    for i in (0, 1, 3):
+    for i in range(3):
         fetches[i].wait()
 
     def extend(step, _):
@@ -120,8 +112,9 @@
 
     each = tgt_blocks // 8 // Y_PARTS
     for i in range(Y_PARTS):
-        fetches[4 + i].wait()
-        lax.fori_loop(i * each, (i + 1) * each, extend, 0)
+        fetches[3 + i].wait()
+        lax.fori_loop(i * each, (i + 1) * each, extend, 0, unroll=2)
+    fetches[3 + Y_PARTS].wait()
     height = left_ref.shape[1]
     first = lax.broadcasted_iota(jnp.int32, (height, BLK), 0) == 2 * features
     left_ref[tgt_blocks] = jnp.where(first, NEG, 0.0).astype(BF16)
@@ -135,7 +128,8 @@
 
     def begin(r):
         lefts = [left_ref[jnp.where(k < counts_ref[r], support_ref[k, 0, r], tgt_blocks)] for k in range(slots)]
-        return jnp.split(tile_score(jnp.concatenate(lefts, axis=1), right_ref[r]), slots, axis=0)
+        right = jnp.concatenate([*split_source(lane_block(x_ref, r), TO_LOG2 / features), ones], axis=0)
+        return jnp.split(tile_score(jnp.concatenate(lefts, axis=1), right), slots, axis=0)
 
     def end(q):
         sums = [tile_sums(score_ref[q * slots + k]) for k in range(slots)]
@@ -429,7 +423,6 @@
             pltpu.VMEM(y.shape, BF16),
             pltpu.VMEM(g.shape, F32),
             pltpu.VMEM((g.shape[0] + 1, 2 * x.shape[0] + 32, BLK), BF16),
-            pltpu.VMEM((blocks, 2 * x.shape[0] + 32, BLK), BF16),
             pltpu.VMEM((BUNCH * slots, BLK, BLK), F32),
             pltpu.VMEM((rows * 8, BLK), F32),
             pltpu.VMEM((rows * 8, BLK), F32),

time: 60.2 us -> 59.5 us (0.988)
  Pallas kernels: 57.7 us -> 57 us
    pallas_call x1, Pallas kernels: 26.1 us -> 25.1 us  [row_pass(): pl.pallas_call(functools.partial(row_kernel, axis, n), out_shape=jax.Shap...]
where the time goes in v8:
time: 59.5 us; the launch traced here: 59.3 us
  Pallas kernels  57 us (96%)
  local copies, waits for them, and re-layouts  1.57 us (3%)
  between operations  0.73 us (1%)
    pallas_call x1, Pallas kernels, row_pass(): pl.pallas_call(functools.partial(row_kernel, axis, n), out_shape=jax.Shap...  25.1 us
    pallas_call x1, Pallas kernels, col_exchange(): pl.pallas_call(functools.partial(col_exchange_kernel, axis, n, shift), ou...  20.3 us
    pallas_call x1, Pallas kernels, col_pass(): pl.pallas_call(functools.partial(col_kernel, log_total), out_shape=(jax.S...  11.7 us
    unnamed x11, local copies, waits for them, and re-layouts  1.57 us

profile of v8, /device:TPU:1, one launch (start us, length us, event | category | flops | bytes accessed | tf_op | source)
XLA Modules:
  0.0 59.3 jit_solution(4985409505136217281)
XLA Ops:
  0.6 0.0 copy-start
  0.6 0.0 copy-start.1
  0.7 0.0 copy-start.4
  0.7 0.0 copy-start.3
  0.7 25.1 %row_pass.1.lse_ref = f32[128,128]{1,0:T(8,128)} custom-call(s32[6,1,128]{2,1,0:T(1,128)} %bitcast.6, s32[128]{0:T(128)} %bitcast.8, bf16[32,16384]{1,0:T(8,128)(2,1)} %x_ref.1, bf16[32,65536]{1,0:T(8,128)(2,1)} %y_any.3, f32[512,128]{1,0:T(8,128)} %bitcast.10), custom_call_target="tpu_custom_call" | custom-call | tf_op jit(solution)/shard_map/row_pass/pallas_call | solution.py:414
  25.7 0.0 copy-done
  25.8 0.0 copy-done.1
  25.8 0.0 copy-done.4
  25.8 0.0 copy-done.3
  25.8 0.0 copy-start.2
  25.8 0.8 %copy-done.2 = f32[128,128]{1,0:T(8,128)S(1)} copy-done((f32[128,128]{1,0:T(8,128)S(1)}, f32[128,128]{1,0:T(8,128)}, u32[]{:S(2)}) %copy-start.2) | copy-done | bytes 65560
  26.6 11.7 %col_pass.1 = (f32[128,128]{1,0:T(8,128)}, f32[512,128]{1,0:T(8,128)S(1)}) custom-call(s32[6,1,128]{2,1,0:T(1,128)S(1)} %bitcast.7, s32[128]{0:T(128)S(1)} %bitcast.9, bf16[32,16384]{1,0:T(8,128)(2,1)S(1)} %copy-done.1, bf16[32,65536]{1,0:T(8,128)(2,1)S(1)} %copy-done, f32[128,128]{1,0:T(8,128)S(1)} %copy-done.2), custom_call_target="tpu_custom_call" | custom-call | tf_op jit(solution)/shard_map/col_pass/pallas_call | solution.py:445
  38.3 20.3 %exchange_src.1 = f32[512,128]{1,0:T(8,128)S(1)} custom-call(f32[512,128]{1,0:T(8,128)S(1)} %get-tuple-element.5.part_any, bf16[32,65536]{1,0:T(8,128)(2,1)S(1)} %copy-done), custom_call_target="tpu_custom_call" | custom-call | tf_op jit(solution)/shard_map/exchange_src/pallas_call | solution.py:386
  58.6 0.7 %copy.8 = f32[65536]{0:T(1024)} copy(f32[65536]{0:T(1024)S(1)} %bitcast.5) | data formatting | bytes 524288
Async XLA Ops:
  0.6 25.1 %copy-start = (bf16[32,65536]{1,0:T(8,128)(2,1)S(1)}, bf16[32,65536]{1,0:T(8,128)(2,1)}, u32[]{:S(2)}) copy-start(bf16[32,65536]{1,0:T(8,128)(2,1)} %y_any.3) | copy-start | bytes 12582916
  0.6 25.1 %copy-start.1 = (bf16[32,16384]{1,0:T(8,128)(2,1)S(1)}, bf16[32,16384]{1,0:T(8,128)(2,1)}, u32[]{:S(2)}) copy-start(bf16[32,16384]{1,0:T(8,128)(2,1)} %x_ref.1) | copy-start | bytes 3145732
  0.7 25.1 %copy-start.4 = (s32[128,1]{0,1:T(1,128)S(1)}, s32[128,1]{0,1:T(1,128)}, u32[]{:S(2)}) copy-start(s32[128,1]{0,1:T(1,128)} %param.9) | copy-start | bytes 1540
  0.7 25.1 %copy-start.3 = (s32[128,1,6]{0,1,2:T(1,128)S(1)}, s32[128,1,6]{0,1,2:T(1,128)}, u32[]{:S(2)}) copy-start(s32[128,1,6]{0,1,2:T(1,128)} %param.8) | copy-start | bytes 9220
  25.8 0.8 %copy-start.2 = (f32[128,128]{1,0:T(8,128)S(1)}, f32[128,128]{1,0:T(8,128)}, u32[]{:S(2)}) copy-start(f32[128,128]{1,0:T(8,128)} %row_pass.1.lse_ref) | copy-start | bytes 196612

commit v9 on v8

--- a/solution.py
+++ b/solution.py
@@ -113,7 +113,7 @@
     each = tgt_blocks // 8 // Y_PARTS
     for i in range(Y_PARTS):
         fetches[3 + i].wait()
-        lax.fori_loop(i * each, (i + 1) * each, extend, 0, unroll=2)
+        lax.fori_loop(i * each, (i + 1) * each, extend, 0, unroll=4)
     fetches[3 + Y_PARTS].wait()
     height = left_ref.shape[1]
     first = lax.broadcasted_iota(jnp.int32, (height, BLK), 0) == 2 * features
@@ -301,7 +301,7 @@
     return high + jnp.log2(sum(jnp.exp2(term - high) for term in terms))
 
 
-PIECES = 4
+PIECES = 2
 
 
 def col_exchange_kernel(axis, n, shift, part_any, y_any, out_ref, mine_ref, twin_ref, pair_ref, parts, whole, y_ref, sq_ref, local_sem, send_a, recv_a, send_b, recv_b, send_c, recv_c, send_d, recv_d):
@@ -372,9 +372,12 @@
         third[s].wait_recv()
         came = chunk(core, senders[s])
         fourth.append(remote(whole.at[came], whole.at[came], send_d.at[s], recv_d.at[s], axis, twin))
+    own_half = pl.ds(pl.multiple_of(core * half, half), half)
+    twin_half = pl.ds(pl.multiple_of((1 - core) * half, half), half)
+    out_ref[own_half, :] = whole[own_half, :]
     for copy in fourth:
         copy.wait_recv()
-    out_ref[...] = whole[...]
+    out_ref[twin_half, :] = whole[twin_half, :]
     for copy in first + second + third + fourth:
         copy.wait_send()
 

time: 59.5 us -> 59.6 us (level)
    pallas_call x1, Pallas kernels: 20.3 us -> 21.6 us  [col_exchange(): pl.pallas_call(functools.partial(col_exchange_kernel, axis, n, shift), ou...]
    pallas_call x1, Pallas kernels: 11.7 us -> 10.8 us  [col_pass(): pl.pallas_call(functools.partial(col_kernel, log_total), out_shape=(jax.S...]
where the time goes in v9:
time: 59.6 us; the launch traced here: 59.5 us
  Pallas kernels  57.2 us (96%)
  local copies, waits for them, and re-layouts  1.57 us (3%)
  between operations  0.73 us (1%)
    pallas_call x1, Pallas kernels, row_pass(): pl.pallas_call(functools.partial(row_kernel, axis, n), out_shape=jax.Shap...  24.8 us
    pallas_call x1, Pallas kernels, col_exchange(): pl.pallas_call(functools.partial(col_exchange_kernel, axis, n, shift), ou...  21.6 us
    pallas_call x1, Pallas kernels, col_pass(): pl.pallas_call(functools.partial(col_kernel, log_total), out_shape=(jax.S...  10.8 us
    unnamed x11, local copies, waits for them, and re-layouts  1.57 us

profile of v9, /device:TPU:1, one launch (start us, length us, event | category | flops | bytes accessed | tf_op | source)
XLA Modules:
  0.0 59.5 jit_solution(18135818255202903392)
XLA Ops:
  0.6 0.0 copy-start
  0.6 0.0 copy-start.1
  0.7 0.0 copy-start.4
  0.7 0.0 copy-start.3
  0.7 24.8 %row_pass.1.lse_ref = f32[128,128]{1,0:T(8,128)} custom-call(s32[6,1,128]{2,1,0:T(1,128)} %bitcast.6, s32[128]{0:T(128)} %bitcast.8, bf16[32,16384]{1,0:T(8,128)(2,1)} %x_ref.1, bf16[32,65536]{1,0:T(8,128)(2,1)} %y_any.3, f32[512,128]{1,0:T(8,128)} %bitcast.10), custom_call_target="tpu_custom_call" | custom-call | tf_op jit(solution)/shard_map/row_pass/pallas_call | solution.py:417
  25.5 0.0 copy-done
  25.5 0.0 copy-done.1
  25.5 0.0 copy-done.4
  25.5 0.0 copy-done.3
  25.5 0.0 copy-start.2
  25.5 0.8 %copy-done.2 = f32[128,128]{1,0:T(8,128)S(1)} copy-done((f32[128,128]{1,0:T(8,128)S(1)}, f32[128,128]{1,0:T(8,128)}, u32[]{:S(2)}) %copy-start.2) | copy-done | bytes 65560
  26.4 10.8 %col_pass.1 = (f32[128,128]{1,0:T(8,128)}, f32[512,128]{1,0:T(8,128)S(1)}) custom-call(s32[6,1,128]{2,1,0:T(1,128)S(1)} %bitcast.7, s32[128]{0:T(128)S(1)} %bitcast.9, bf16[32,16384]{1,0:T(8,128)(2,1)S(1)} %copy-done.1, bf16[32,65536]{1,0:T(8,128)(2,1)S(1)} %copy-done, f32[128,128]{1,0:T(8,128)S(1)} %copy-done.2), custom_call_target="tpu_custom_call" | custom-call | tf_op jit(solution)/shard_map/col_pass/pallas_call | solution.py:448
  37.1 21.6 %exchange_src.1 = f32[512,128]{1,0:T(8,128)S(1)} custom-call(f32[512,128]{1,0:T(8,128)S(1)} %get-tuple-element.5.part_any, bf16[32,65536]{1,0:T(8,128)(2,1)S(1)} %copy-done), custom_call_target="tpu_custom_call" | custom-call | tf_op jit(solution)/shard_map/exchange_src/pallas_call | solution.py:389
  58.8 0.7 %copy.8 = f32[65536]{0:T(1024)} copy(f32[65536]{0:T(1024)S(1)} %bitcast.5) | data formatting | bytes 524288
Async XLA Ops:
  0.6 24.9 %copy-start = (bf16[32,65536]{1,0:T(8,128)(2,1)S(1)}, bf16[32,65536]{1,0:T(8,128)(2,1)}, u32[]{:S(2)}) copy-start(bf16[32,65536]{1,0:T(8,128)(2,1)} %y_any.3) | copy-start | bytes 12582916
  0.6 24.9 %copy-start.1 = (bf16[32,16384]{1,0:T(8,128)(2,1)S(1)}, bf16[32,16384]{1,0:T(8,128)(2,1)}, u32[]{:S(2)}) copy-start(bf16[32,16384]{1,0:T(8,128)(2,1)} %x_ref.1) | copy-start | bytes 3145732
  0.7 24.9 %copy-start.4 = (s32[128,1]{0,1:T(1,128)S(1)}, s32[128,1]{0,1:T(1,128)}, u32[]{:S(2)}) copy-start(s32[128,1]{0,1:T(1,128)} %param.9) | copy-start | bytes 1540
  0.7 24.9 %copy-start.3 = (s32[128,1,6]{0,1,2:T(1,128)S(1)}, s32[128,1,6]{0,1,2:T(1,128)}, u32[]{:S(2)}) copy-start(s32[128,1,6]{0,1,2:T(1,128)} %param.8) | copy-start | bytes 9220
  25.5 0.8 %copy-start.2 = (f32[128,128]{1,0:T(8,128)S(1)}, f32[128,128]{1,0:T(8,128)}, u32[]{:S(2)}) copy-start(f32[128,128]{1,0:T(8,128)} %row_pass.1.lse_ref) | copy-start | bytes 196612

commit v10 on v9

--- a/solution.py
+++ b/solution.py
@@ -113,7 +113,7 @@
     each = tgt_blocks // 8 // Y_PARTS
     for i in range(Y_PARTS):
         fetches[3 + i].wait()
-        lax.fori_loop(i * each, (i + 1) * each, extend, 0, unroll=4)
+        lax.fori_loop(i * each, (i + 1) * each, extend, 0, unroll=8)
     fetches[3 + Y_PARTS].wait()
     height = left_ref.shape[1]
     first = lax.broadcasted_iota(jnp.int32, (height, BLK), 0) == 2 * features
@@ -301,7 +301,7 @@
     return high + jnp.log2(sum(jnp.exp2(term - high) for term in terms))
 
 
-PIECES = 2
+PIECES = 1
 
 
 def col_exchange_kernel(axis, n, shift, part_any, y_any, out_ref, mine_ref, twin_ref, pair_ref, parts, whole, y_ref, sq_ref, local_sem, send_a, recv_a, send_b, recv_b, send_c, recv_c, send_d, recv_d):

time: 59.6 us -> 59.6 us (level)
    pallas_call x1, Pallas kernels: 10.8 us -> 11.7 us  [col_pass(): pl.pallas_call(functools.partial(col_kernel, log_total), out_shape=(jax.S...]
    pallas_call x1, Pallas kernels: 21.6 us -> 20.8 us  [col_exchange(): pl.pallas_call(functools.partial(col_exchange_kernel, axis, n, shift), ou...]
where the time goes in v10:
time: 59.6 us; the launch traced here: 59.5 us
  Pallas kernels  57.2 us (96%)
  local copies, waits for them, and re-layouts  1.57 us (3%)
  between operations  0.73 us (1%)
    pallas_call x1, Pallas kernels, row_pass(): pl.pallas_call(functools.partial(row_kernel, axis, n), out_shape=jax.Shap...  24.7 us
    pallas_call x1, Pallas kernels, col_exchange(): pl.pallas_call(functools.partial(col_exchange_kernel, axis, n, shift), ou...  20.8 us
    pallas_call x1, Pallas kernels, col_pass(): pl.pallas_call(functools.partial(col_kernel, log_total), out_shape=(jax.S...  11.7 us
    unnamed x11, local copies, waits for them, and re-layouts  1.57 us

profile of v10, /device:TPU:1, one launch (start us, length us, event | category | flops | bytes accessed | tf_op | source)
XLA Modules:
  0.0 59.5 jit_solution(8984939986373622372)
XLA Ops:
  0.6 0.0 copy-start
  0.6 0.0 copy-start.1
  0.7 0.0 copy-start.4
  0.7 0.0 copy-start.3
  0.7 24.7 %row_pass.1.lse_ref = f32[128,128]{1,0:T(8,128)} custom-call(s32[6,1,128]{2,1,0:T(1,128)} %bitcast.6, s32[128]{0:T(128)} %bitcast.8, bf16[32,16384]{1,0:T(8,128)(2,1)} %x_ref.1, bf16[32,65536]{1,0:T(8,128)(2,1)} %y_any.3, f32[512,128]{1,0:T(8,128)} %bitcast.10), custom_call_target="tpu_custom_call" | custom-call | tf_op jit(solution)/shard_map/row_pass/pallas_call | solution.py:417
  25.4 0.0 copy-done
  25.4 0.0 copy-done.1
  25.4 0.0 copy-done.4
  25.4 0.0 copy-done.3
  25.4 0.0 copy-start.2
  25.4 0.8 %copy-done.2 = f32[128,128]{1,0:T(8,128)S(1)} copy-done((f32[128,128]{1,0:T(8,128)S(1)}, f32[128,128]{1,0:T(8,128)}, u32[]{:S(2)}) %copy-start.2) | copy-done | bytes 65560
  26.3 11.7 %col_pass.1 = (f32[128,128]{1,0:T(8,128)}, f32[512,128]{1,0:T(8,128)S(1)}) custom-call(s32[6,1,128]{2,1,0:T(1,128)S(1)} %bitcast.7, s32[128]{0:T(128)S(1)} %bitcast.9, bf16[32,16384]{1,0:T(8,128)(2,1)S(1)} %copy-done.1, bf16[32,65536]{1,0:T(8,128)(2,1)S(1)} %copy-done, f32[128,128]{1,0:T(8,128)S(1)} %copy-done.2), custom_call_target="tpu_custom_call" | custom-call | tf_op jit(solution)/shard_map/col_pass/pallas_call | solution.py:448
  38.0 20.8 %exchange_src.1 = f32[512,128]{1,0:T(8,128)S(1)} custom-call(f32[512,128]{1,0:T(8,128)S(1)} %get-tuple-element.5.part_any, bf16[32,65536]{1,0:T(8,128)(2,1)S(1)} %copy-done), custom_call_target="tpu_custom_call" | custom-call | tf_op jit(solution)/shard_map/exchange_src/pallas_call | solution.py:389
  58.8 0.7 %copy.8 = f32[65536]{0:T(1024)} copy(f32[65536]{0:T(1024)S(1)} %bitcast.5) | data formatting | bytes 524288
Async XLA Ops:
  0.6 24.8 %copy-start = (bf16[32,65536]{1,0:T(8,128)(2,1)S(1)}, bf16[32,65536]{1,0:T(8,128)(2,1)}, u32[]{:S(2)}) copy-start(bf16[32,65536]{1,0:T(8,128)(2,1)} %y_any.3) | copy-start | bytes 12582916
  0.6 24.8 %copy-start.1 = (bf16[32,16384]{1,0:T(8,128)(2,1)S(1)}, bf16[32,16384]{1,0:T(8,128)(2,1)}, u32[]{:S(2)}) copy-start(bf16[32,16384]{1,0:T(8,128)(2,1)} %x_ref.1) | copy-start | bytes 3145732
  0.7 24.8 %copy-start.4 = (s32[128,1]{0,1:T(1,128)S(1)}, s32[128,1]{0,1:T(1,128)}, u32[]{:S(2)}) copy-start(s32[128,1]{0,1:T(1,128)} %param.9) | copy-start | bytes 1540
  0.7 24.8 %copy-start.3 = (s32[128,1,6]{0,1,2:T(1,128)S(1)}, s32[128,1,6]{0,1,2:T(1,128)}, u32[]{:S(2)}) copy-start(s32[128,1,6]{0,1,2:T(1,128)} %param.8) | copy-start | bytes 9220
  25.4 0.8 %copy-start.2 = (f32[128,128]{1,0:T(8,128)S(1)}, f32[128,128]{1,0:T(8,128)}, u32[]{:S(2)}) copy-start(f32[128,128]{1,0:T(8,128)} %row_pass.1.lse_ref) | copy-start | bytes 196612
